TPU v7x, 128 devices: a whole 4x4x4 slice. The times are simulated.
128 devices in a mesh: rows: 16 (over y, z), cols: 8 (over x, core).
Axes of the slice: x: 4, y: 4, z: 4, core: 2. Of those that a mesh axis runs over, the one named last changes fastest.
Arguments:
- tile_values: float32 [16, 8, 320, 128, 128], P('rows', 'cols'), may hold values from -3.2 to 3.2
- tile_rows: int32 [16, 8, 320], P('rows', 'cols'), may hold values from 0 to 63
- tile_cols: int32 [16, 8, 320], P('rows', 'cols'), may hold values from 0 to 127
- tile_count: int32 [16, 8], P('rows', 'cols'), may hold values from 1 to 320, as said below
- probes: float32 [131072, 128], P(('rows', 'cols')), may hold values from -6.1 to 6.1
Outputs:
- basis: float32 [131072, 128], P(('rows', 'cols'))
- factor: float32 [128, 128], replicated
- first_factor: float32 [128, 128], replicated
Inputs may be any that keep to these rules, and one draw needn't show every extreme that they name: `tile_count`: counts are skewed; at least one device has all 320 slots live in every draw.
All inputs are finite; a program needn't handle non-finite values.
Results may differ from a plain program's by a relative error of at most 0.0005.
Values sent between devices are 32-bit elements; how exact they have to be, the bound alone decides.
A program may use at most 192 MiB of HBM per device.

v0:
```python
import jax
import jax.numpy as jnp
from jax import lax
from jax.sharding import PartitionSpec as P


def panel_partial(tiles, rows_idx, cols_idx, count, columns, panel_blocks):
    tile_size = tiles.shape[1]
    width = columns.shape[1]
    blocks = columns.reshape(-1, tile_size, width)
    picked = jnp.take(blocks, cols_idx, axis=0)
    products = jnp.einsum("cij,cjk->cik", tiles, picked, precision=lax.Precision.HIGHEST)
    slots = jnp.arange(tiles.shape[0], dtype=jnp.int32)
    live = slots < count
    onehot = (
        (rows_idx[None, :] == jnp.arange(panel_blocks, dtype=jnp.int32)[:, None]) & live[None, :]
    ).astype(tiles.dtype)
    return jnp.einsum("pc,cik->pik", onehot, products, precision=lax.Precision.HIGHEST).reshape(
        -1, width
    )


def local_gram(matrix):
    return jnp.einsum("rk,rl->kl", matrix, matrix, precision=lax.Precision.HIGHEST)


def triangle_inverse(gram, nodes):
    lower = jnp.linalg.cholesky(gram / nodes)
    inverse = jax.scipy.linalg.solve_triangular(
        lower, jnp.eye(gram.shape[0], dtype=gram.dtype), lower=True
    )
    return (lower, inverse)


def shards(tile_values, tile_rows, tile_cols, tile_count, probes):
    tiles = tile_values[0, 0]
    rows_idx = tile_rows[0, 0]
    cols_idx = tile_cols[0, 0]
    count = tile_count[0, 0]
    own_rows = probes.shape[0]
    tile_size = tiles.shape[1]
    nodes = own_rows * lax.axis_size("rows") * lax.axis_size("cols")
    panel_blocks = lax.axis_size("cols") * own_rows // tile_size
    gathered = lax.all_gather(probes, "rows", axis=0, tiled=True)
    panel = panel_partial(tiles, rows_idx, cols_idx, count, gathered, panel_blocks)
    own = lax.psum_scatter(panel, "cols", scatter_dimension=0, tiled=True)
    gram = lax.psum(local_gram(own), ("rows", "cols"))
    lower, inverse = triangle_inverse(gram, nodes)
    first = jnp.dot(own, inverse.T, precision=lax.Precision.HIGHEST)
    gram_next = lax.psum(local_gram(first), ("rows", "cols"))
    lower_next, inverse_next = triangle_inverse(gram_next, nodes)
    basis = jnp.dot(first, inverse_next.T, precision=lax.Precision.HIGHEST)
    factor = jnp.dot(lower_next.T, lower.T, precision=lax.Precision.HIGHEST)
    return (basis, factor, lower.T)


def solution(mesh):
    placed = (
        P("rows", "cols", None, None, None),
        P("rows", "cols", None),
        P("rows", "cols", None),
        P("rows", "cols"),
        P(("rows", "cols"), None),
    )
    return jax.shard_map(
        shards,
        mesh=mesh,
        in_specs=placed,
        out_specs=(P(("rows", "cols"), None), P(), P()),
        check_vma=False,
    )
```

profile of v0, /device:TPU:1, one launch (start us, length us, event | category | flops | bytes accessed | tf_op | source)
XLA Modules:
  0.0 563.5 jit_solution(11547567714651964568)
XLA Ops:
  7.2 0.0 all-gather.2.cloned.1.call-start
  7.2 0.7 all-gather.2.cloned.1.call-update
  7.9 0.0 reduce-scatter.2.cloned.1.call-start
  7.9 0.7 reduce.5
  8.6 0.7 reduce.4
  10.0 0.7 fusion.28
  10.7 73.5 %all-gather.2.cloned.1.call-done = f32[16384,128]{1,0:T(8,128)} async-done(((f32[1024,128]{1,0:T(8,128)}), f32[16384,128]{1,0:T(8,128)}) %all-gather.2.cloned.1.call-update) | async-done | bytes 8388624 | tf_op jit(solution)/shard_map/all_gather | solution.py:44
  84.3 17.2 %gather_fusion = f32[320,128,128]{2,1,0:T(8,128)} fusion(f32[128,128,128]{2,1,0:T(8,128)} %bitcast.43, s32[1024]{0:T(1024)S(1)} %pad_clamp_fusion), kind=kCustom, calls=%fused_computation | custom fusion | bytes 41944320 | tf_op jit(solution)/shard_map/jit(_take)/gather | solution.py:11
  101.4 45.0 %fusion.2 = f32[320,128,128]{2,1,0:T(8,128)} fusion(f32[1,1,320,128,128]{4,3,2,1,0:T(8,128)} %param.8, f32[320,128,128]{2,1,0:T(8,128)} %gather_fusion, pred[320]{0:T(512)(128)(4,1)S(1)} %compare_and_fusion), kind=kOutput, calls=%fused_computation.3 | convolution fusion | flops 8058306560 | bytes 62914880 | tf_op jit(solution)/shard_map/cij,cjk->cik/dot_general | solution.py:12
  146.4 21.4 %copy.19 = f32[320,128,128]{1,0,2:T(8,128)} copy(f32[320,128,128]{2,1,0:T(8,128)} %fusion.2) | data formatting | bytes 41943040 | tf_op jit(solution)/shard_map/cij,cjk->cik/dot_general | solution.py:12
  167.9 13.4 %fusion = f32[64,128,128]{2,0,1:T(8,128)S(1)} fusion(f32[320,128,128]{1,0,2:T(8,128)} %copy.19, s32[320]{0:T(512)S(1)} %reduce.4, pred[320]{0:T(512)(128)(4,1)S(1)} %iota_compare_fusion.5), kind=kOutput, calls=%fused_computation.1 | convolution fusion | flops 4026572800 | bytes 25167424 | tf_op jit(solution)/shard_map/pc,cik->pik/dot_general | solution.py:18
  181.3 4.4 copy.13
  185.7 0.0 reduce-scatter.2.cloned.1.call-update
  185.7 0.0 all-reduce.3.cloned.1.call-start
  185.7 34.6 %reduce-scatter.2.cloned.1.call-done = f32[1024,128]{1,0:T(8,128)} async-done(((f32[8192,128]{1,0:T(8,128)}), f32[1024,128]{1,0:T(8,128)}) %reduce-scatter.2.cloned.1.call-update) | async-done | bytes 524304 | tf_op jit(solution)/shard_map/reduce_scatter | solution.py:46
  220.4 2.8 fusion.32
  223.2 0.0 all-reduce.3.cloned.1.call-update
  223.2 0.3 all-reduce.5.cloned.1.call-start
  223.5 141.8 %all-reduce.3.cloned.1.call-done = f32[128,128]{0,1:T(8,128)} async-done(((f32[128,128]{0,1:T(8,128)}), f32[128,128]{0,1:T(8,128)}) %all-reduce.3.cloned.1.call-update) | async-done | bytes 65552 | tf_op jit(solution)/shard_map/psum | solution.py:47
  365.3 0.8 broadcast_multiply_fusion.1
  366.1 0.1 copy.15
  366.2 0.9 fusion.17
  367.1 11.7 %cholesky.44 = f32[128,128]{1,0:T(8,128)S(1)} custom-call(f32[128,128]{1,0:T(8,128)S(1)} %fusion.17), custom_call_target="Cholesky" | custom-call | tf_op jit(solution)/shard_map/jit(cholesky)/cholesky | solution.py:28
  378.8 0.6 compare_reduce_fusion.1
  379.5 0.7 fusion.22
  380.1 9.8 %custom-call.6 = f32[1,128,128]{1,2,0:T(8,128)S(1)} custom-call(f32[1,128,128]{2,1,0:T(8,128)S(1)} %get-tuple-element.12), custom_call_target="InvertDiagBlocksLowerTriangular" | custom-call | tf_op jit(solution)/shard_map/jit(_solve_triangular)/triangular_solve | solution.py:29
  390.0 0.3 fusion.12
  390.2 1.6 fusion.33
  391.9 1.6 fusion.34
  393.5 0.0 all-reduce.5.cloned.1.call-update
  393.5 0.7 copy.18
  394.3 134.0 %all-reduce.5.cloned.1.call-done = f32[128,128]{0,1:T(8,128)} async-done(((f32[128,128]{0,1:T(8,128)}), f32[128,128]{0,1:T(8,128)}) %all-reduce.5.cloned.1.call-update) | async-done | bytes 65552 | tf_op jit(solution)/shard_map/psum | solution.py:50
  528.3 0.8 broadcast_multiply_fusion
  529.1 0.1 copy.17
  529.2 0.9 fusion.15
  530.1 11.7 %cholesky.55 = f32[128,128]{1,0:T(8,128)S(1)} custom-call(f32[128,128]{1,0:T(8,128)S(1)} %fusion.15), custom_call_target="Cholesky" | custom-call | tf_op jit(solution)/shard_map/jit(cholesky)/cholesky | solution.py:28
  541.8 0.7 compare_reduce_fusion
  542.6 2.3 fusion.19
  544.8 0.7 select_bitcast_fusion
  545.5 9.8 %custom-call.7 = f32[1,128,128]{1,2,0:T(8,128)S(1)} custom-call(f32[1,128,128]{2,1,0:T(8,128)S(1)} %select_bitcast_fusion), custom_call_target="InvertDiagBlocksLowerTriangular" | custom-call | tf_op jit(solution)/shard_map/jit(_solve_triangular)/triangular_solve | solution.py:29
  555.3 0.3 fusion.10
  555.6 1.4 fusion.35
  (5 shorter events, 0.1 us)
Async XLA Ops:
  7.2 77.1 %all-gather.2.cloned.1.call-start = ((), (), s32[]{:S(2)}) async-start(), calls=%async_computation.1 | async-start | bytes 8912896 | tf_op jit(solution)/shard_map/all_gather | solution.py:44
  7.9 212.5 %reduce-scatter.2.cloned.1.call-start = ((), (), s32[]{:S(2)}) async-start(), calls=%async_computation.2 | async-start | bytes 4718592 | tf_op jit(solution)/shard_map/reduce_scatter | solution.py:46
  185.7 179.6 %all-reduce.3.cloned.1.call-start = ((), (), s32[]{:S(2)}) async-start(), calls=%async_computation.3 | async-start | bytes 131072 | tf_op jit(solution)/shard_map/psum | solution.py:47
  223.2 305.1 %all-reduce.5.cloned.1.call-start = ((), (), s32[]{:S(2)}) async-start(), calls=%async_computation.4 | async-start | bytes 131072 | tf_op jit(solution)/shard_map/psum | solution.py:50
Sparse Core Ops, SparseCore 0:
  10.1 74.0 all-gather.1
  185.8 34.5 reduce-scatter.1
  225.7 139.5 all-reduce.2
  393.7 134.5 all-reduce.4
where the time goes:
time: 564 us
  waiting for transfers between devices  385 us (68%)
  matrix products  68.7 us (12%)
  other arithmetic  51.4 us (9%)
  local copies, waits for them, and re-layouts  43.9 us (8%)
  between operations  14.5 us (3%)
    psum x1, waiting for transfers between devices, shards(): gram = lax.psum(local_gram(own), ('rows', 'cols'))  142 us
    psum x1, waiting for transfers between devices, shards(): gram_next = lax.psum(local_gram(first), ('rows', 'cols'))  134 us
    all_gather x1, waiting for transfers between devices, shards(): gathered = lax.all_gather(probes, 'rows', axis=0, tiled=True)  73.5 us
    dot_general x1, matrix products, panel_partial(): jnp.einsum('cij,cjk->cik', tiles, picked, precision=lax.Precision.HIGHEST)  45 us
    reduce_scatter x1, waiting for transfers between devices, shards(): own = lax.psum_scatter(panel, 'cols', scatter_dimension=0, tiled=True)  34.6 us
    another operation x6, other arithmetic, triangle_inverse(): lower = jnp.linalg.cholesky(gram / nodes)  24.9 us
    dot_general x1, local copies, waits for them, and re-layouts, panel_partial(): jnp.einsum('cij,cjk->cik', tiles, picked, precision=lax.Precision.HIGHEST)  21.4 us
    another operation x3, other arithmetic, triangle_inverse(): jax.scipy.linalg.solve_triangular(lower, jnp.eye(gram.shape[0], dtype=gra...  20.3 us
  transfers between devices with their start and end apart: 4, of which 4 were waited for; matrix products, arithmetic and copies ran while one was open for 1% of the time, Pallas kernels for 0%

commit v1 on v0

--- a/solution.py
+++ b/solution.py
@@ -1,7 +1,13 @@
 import jax
 import jax.numpy as jnp
 from jax import lax
+from jax.experimental import pallas as pl
+from jax.experimental.pallas import tpu as pltpu
 from jax.sharding import PartitionSpec as P
+
+N_ROWS = 16
+N_COLS = 8
+MESH = pl.DeviceIdType.MESH
 
 
 def panel_partial(tiles, rows_idx, cols_idx, count, columns, panel_blocks):
@@ -32,6 +38,89 @@
     return (lower, inverse)
 
 
+def signal_all(sem, r, c):
+    def cols_peer(d, carry):
+        pl.semaphore_signal(sem, inc=1, device_id=(r, lax.rem(c + d, N_COLS)), device_id_type=MESH)
+        return carry
+
+    def rows_peer(d, carry):
+        pl.semaphore_signal(sem, inc=1, device_id=(lax.rem(r + d, N_ROWS), c), device_id_type=MESH)
+        return carry
+
+    lax.fori_loop(1, N_COLS, cols_peer, 0)
+    lax.fori_loop(1, N_ROWS, rows_peer, 0)
+
+
+def sum_kernel(g_ref, out_ref, part, got_a, got_b, send_a, recv_a, send_b, recv_b, send_c, recv_c):
+    r, c = lax.axis_index("rows"), lax.axis_index("cols")
+    barrier = pltpu.get_barrier_semaphore()
+    signal_all(barrier, r, c)
+    pl.semaphore_wait(barrier, N_COLS - 1 + N_ROWS - 1)
+
+    def copy_a(d):
+        to = lax.rem(c + d, N_COLS)
+        return pltpu.make_async_remote_copy(
+            src_ref=g_ref.at[to], dst_ref=got_a.at[d], send_sem=send_a.at[d], recv_sem=recv_a.at[d],
+            device_id=(r, to), device_id_type=MESH)
+
+    def copy_b(d):
+        return pltpu.make_async_remote_copy(
+            src_ref=part, dst_ref=got_b.at[r], send_sem=send_b.at[d], recv_sem=recv_b.at[d],
+            device_id=(lax.rem(r + d, N_ROWS), c), device_id_type=MESH)
+
+    def copy_c(d):
+        return pltpu.make_async_remote_copy(
+            src_ref=out_ref.at[c], dst_ref=out_ref.at[c], send_sem=send_c.at[d], recv_sem=recv_c.at[d],
+            device_id=(r, lax.rem(c + d, N_COLS)), device_id_type=MESH)
+
+    def each(copy, n, act):
+        def step(d, carry):
+            getattr(copy(d), act)()
+            return carry
+
+        lax.fori_loop(1, n, step, 0)
+
+    each(copy_a, N_COLS, "start")
+    each(copy_a, N_COLS, "wait_recv")
+    total = g_ref[c]
+    for d in range(1, N_COLS):
+        total = total + got_a[d]
+    part[...] = total
+    got_b[r] = total
+    each(copy_b, N_ROWS, "start")
+    each(copy_a, N_COLS, "wait_send")
+    each(copy_b, N_ROWS, "wait_recv")
+    total = got_b[0]
+    for d in range(1, N_ROWS):
+        total = total + got_b[d]
+    out_ref[c] = total
+    each(copy_c, N_COLS, "start")
+    each(copy_b, N_ROWS, "wait_send")
+    each(copy_c, N_COLS, "wait")
+
+
+def sum_everywhere(matrix, ident):
+    size = matrix.shape[0]
+    rows = size // N_COLS
+    piece = (rows, size)
+    dma = pltpu.SemaphoreType.DMA
+    out = pl.pallas_call(
+        sum_kernel,
+        out_shape=jax.ShapeDtypeStruct((N_COLS,) + piece, jnp.float32),
+        in_specs=[pl.BlockSpec(memory_space=pltpu.VMEM)],
+        out_specs=pl.BlockSpec(memory_space=pltpu.VMEM),
+        scratch_shapes=[
+            pltpu.VMEM(piece, jnp.float32),
+            pltpu.VMEM((N_COLS,) + piece, jnp.float32),
+            pltpu.VMEM((N_ROWS,) + piece, jnp.float32),
+            dma((N_COLS,)), dma((N_COLS,)), dma((N_ROWS,)), dma((N_ROWS,)), dma((N_COLS,)), dma((N_COLS,)),
+        ],
+        compiler_params=pltpu.CompilerParams(collective_id=ident, has_side_effects=True),
+        name="sum_everywhere",
+    )(matrix.reshape((N_COLS,) + piece))
+    return out.reshape(size, size)
+
+
 def shards(tile_values, tile_rows, tile_cols, tile_count, probes):
     tiles = tile_values[0, 0]
     rows_idx = tile_rows[0, 0]
@@ -39,15 +128,15 @@
     count = tile_count[0, 0]
     own_rows = probes.shape[0]
     tile_size = tiles.shape[1]
-    nodes = own_rows * lax.axis_size("rows") * lax.axis_size("cols")
-    panel_blocks = lax.axis_size("cols") * own_rows // tile_size
+    nodes = own_rows * N_ROWS * N_COLS
+    panel_blocks = N_COLS * own_rows // tile_size
     gathered = lax.all_gather(probes, "rows", axis=0, tiled=True)
     panel = panel_partial(tiles, rows_idx, cols_idx, count, gathered, panel_blocks)
     own = lax.psum_scatter(panel, "cols", scatter_dimension=0, tiled=True)
-    gram = lax.psum(local_gram(own), ("rows", "cols"))
+    gram = sum_everywhere(local_gram(own), 1)
     lower, inverse = triangle_inverse(gram, nodes)
     first = jnp.dot(own, inverse.T, precision=lax.Precision.HIGHEST)
-    gram_next = lax.psum(local_gram(first), ("rows", "cols"))
+    gram_next = sum_everywhere(local_gram(first), 1)
     lower_next, inverse_next = triangle_inverse(gram_next, nodes)
     basis = jnp.dot(first, inverse_next.T, precision=lax.Precision.HIGHEST)
     factor = jnp.dot(lower_next.T, lower.T, precision=lax.Precision.HIGHEST)

time: 564 us -> 326 us (0.58)
  waiting for transfers between devices: 385 us -> 109 us
  Pallas kernels: 0 us -> 39.8 us
    psum x2 -> x0, waiting for transfers between devices: 276 us -> none  [the longest x1 142 us: shards(): gram = lax.psum(local_gram(own), ('rows', 'cols'))]
    pallas_call x0 -> x2, Pallas kernels: none -> 39.8 us  [sum_everywhere(): pl.pallas_call(sum_kernel, out_shape=jax.ShapeDtypeStruct((N_COLS,) + pie...]
  transfers between devices with their start and end apart: 4 -> 2, of which waited for: 4 -> 2; matrix products, arithmetic and copies ran while one was open for 1% -> 1% of each run, Pallas kernels for 0% -> 0%
where the time goes in v1:
time: 326 us
  waiting for transfers between devices  109 us (33%)
  matrix products  68.7 us (21%)
  other arithmetic  49.5 us (15%)
  local copies, waits for them, and re-layouts  43.9 us (13%)
  Pallas kernels  39.8 us (12%)
  between operations  14.8 us (5%)
    all_gather x1, waiting for transfers between devices, shards(): gathered = lax.all_gather(probes, 'rows', axis=0, tiled=True)  73.5 us
    dot_general x1, matrix products, panel_partial(): jnp.einsum('cij,cjk->cik', tiles, picked, precision=lax.Precision.HIGHEST)  45 us
    pallas_call x2, Pallas kernels, sum_everywhere(): pl.pallas_call(sum_kernel, out_shape=jax.ShapeDtypeStruct((N_COLS,) + pie...  39.8 us
    reduce_scatter x1, waiting for transfers between devices, shards(): own = lax.psum_scatter(panel, 'cols', scatter_dimension=0, tiled=True)  34.6 us
    another operation x6, other arithmetic, triangle_inverse(): lower = jnp.linalg.cholesky(gram / nodes)  24.8 us
    dot_general x1, local copies, waits for them, and re-layouts, panel_partial(): jnp.einsum('cij,cjk->cik', tiles, picked, precision=lax.Precision.HIGHEST)  21.4 us
    another operation x3, other arithmetic, triangle_inverse(): jax.scipy.linalg.solve_triangular(lower, jnp.eye(gram.shape[0], dtype=gra...  20.3 us
    gather x1, local copies, waits for them, and re-layouts, panel_partial(): picked = jnp.take(blocks, cols_idx, axis=0)  17.2 us
  transfers between devices with their start and end apart: 2, of which 2 were waited for; matrix products, arithmetic and copies ran while one was open for 1% of the time, Pallas kernels for 0%

profile of v1, /device:TPU:1, one launch (start us, length us, event | category | flops | bytes accessed | tf_op | source)
XLA Modules:
  0.0 325.6 jit_solution(1150664278948082351)
XLA Ops:
  7.2 0.0 all-gather.2.cloned.1.call-start
  7.2 0.7 all-gather.2.cloned.1.call-update
  7.9 0.0 reduce-scatter.2.cloned.1.call-start
  7.9 0.7 reduce.5
  8.6 0.7 reduce.4
  10.0 0.7 fusion.28
  10.7 73.5 %all-gather.2.cloned.1.call-done = f32[16384,128]{1,0:T(8,128)} async-done(((f32[1024,128]{1,0:T(8,128)}), f32[16384,128]{1,0:T(8,128)}) %all-gather.2.cloned.1.call-update) | async-done | bytes 8388624 | tf_op jit(solution)/shard_map/all_gather | solution.py:133
  84.3 17.2 %gather_fusion = f32[320,128,128]{2,1,0:T(8,128)} fusion(f32[128,128,128]{2,1,0:T(8,128)} %bitcast.49, s32[1024]{0:T(1024)S(1)} %pad_clamp_fusion), kind=kCustom, calls=%fused_computation | custom fusion | bytes 41944320 | tf_op jit(solution)/shard_map/jit(_take)/gather | solution.py:17
  101.4 45.0 %fusion.2 = f32[320,128,128]{2,1,0:T(8,128)} fusion(f32[1,1,320,128,128]{4,3,2,1,0:T(8,128)} %param.8, f32[320,128,128]{2,1,0:T(8,128)} %gather_fusion, pred[320]{0:T(512)(128)(4,1)S(1)} %compare_and_fusion), kind=kOutput, calls=%fused_computation.3 | convolution fusion | flops 8058306560 | bytes 62914880 | tf_op jit(solution)/shard_map/cij,cjk->cik/dot_general | solution.py:18
  146.4 21.4 %copy.16 = f32[320,128,128]{1,0,2:T(8,128)} copy(f32[320,128,128]{2,1,0:T(8,128)} %fusion.2) | data formatting | bytes 41943040 | tf_op jit(solution)/shard_map/cij,cjk->cik/dot_general | solution.py:18
  167.9 13.4 %fusion = f32[64,128,128]{2,0,1:T(8,128)S(1)} fusion(f32[320,128,128]{1,0,2:T(8,128)} %copy.16, s32[320]{0:T(512)S(1)} %reduce.4, pred[320]{0:T(512)(128)(4,1)S(1)} %iota_compare_fusion.5), kind=kOutput, calls=%fused_computation.1 | convolution fusion | flops 4026572800 | bytes 25167424 | tf_op jit(solution)/shard_map/pc,cik->pik/dot_general | solution.py:24
  181.3 4.4 %copy.12 = f32[64,128,128]{2,1,0:T(8,128)} copy(f32[64,128,128]{2,0,1:T(8,128)S(1)} %fusion) | data formatting | bytes 8388608 | tf_op jit(solution)/shard_map/pc,cik->pik/dot_general | solution.py:24
  185.6 0.0 reduce-scatter.2.cloned.1.call-update
  185.7 34.6 %reduce-scatter.2.cloned.1.call-done = f32[1024,128]{1,0:T(8,128)} async-done(((f32[8192,128]{1,0:T(8,128)}), f32[1024,128]{1,0:T(8,128)}) %reduce-scatter.2.cloned.1.call-update) | async-done | bytes 524304 | tf_op jit(solution)/shard_map/reduce_scatter | solution.py:135
  220.3 2.8 fusion.32
  223.1 22.2 %sum_everywhere.2 = f32[8,16,128]{2,1,0:T(8,128)} custom-call(f32[8,16,128]{2,1,0:T(8,128)} %bitcast.53), custom_call_target="tpu_custom_call" | custom-call | tf_op jit(solution)/shard_map/sum_everywhere/pallas_call | solution.py:107
  245.3 0.8 broadcast_multiply_fusion.1
  246.1 0.1 copy.13
  246.2 11.7 %cholesky.44 = f32[128,128]{1,0:T(8,128)S(1)} custom-call(f32[128,128]{1,0:T(8,128)S(1)} %fusion.17), custom_call_target="Cholesky" | custom-call | tf_op jit(solution)/shard_map/jit(cholesky)/cholesky | solution.py:34
  258.0 0.6 compare_reduce_fusion.1
  258.6 0.7 fusion.22
  259.3 9.8 %custom-call.6 = f32[1,128,128]{1,2,0:T(8,128)S(1)} custom-call(f32[1,128,128]{2,1,0:T(8,128)S(1)} %get-tuple-element.12), custom_call_target="InvertDiagBlocksLowerTriangular" | custom-call | tf_op jit(solution)/shard_map/jit(_solve_triangular)/triangular_solve | solution.py:35
  269.1 0.3 fusion.12
  269.4 1.6 fusion.33
  271.0 1.6 fusion.34
  272.7 17.6 %sum_everywhere.3 = f32[8,16,128]{2,1,0:T(8,128)} custom-call(f32[8,16,128]{2,1,0:T(8,128)} %bitcast.54), custom_call_target="tpu_custom_call" | custom-call | tf_op jit(solution)/shard_map/sum_everywhere/pallas_call | solution.py:107
  290.3 0.8 broadcast_multiply_fusion
  291.1 0.1 copy.14
  291.3 11.7 %cholesky.55 = f32[128,128]{1,0:T(8,128)S(1)} custom-call(f32[128,128]{1,0:T(8,128)S(1)} %fusion.15), custom_call_target="Cholesky" | custom-call | tf_op jit(solution)/shard_map/jit(cholesky)/cholesky | solution.py:34
  303.0 0.6 compare_reduce_fusion
  303.6 2.2 fusion.19
  305.9 0.7 select_bitcast_fusion
  306.5 9.8 %custom-call.7 = f32[1,128,128]{1,2,0:T(8,128)S(1)} custom-call(f32[1,128,128]{2,1,0:T(8,128)S(1)} %select_bitcast_fusion), custom_call_target="InvertDiagBlocksLowerTriangular" | custom-call | tf_op jit(solution)/shard_map/jit(_solve_triangular)/triangular_solve | solution.py:35
  316.3 0.3 fusion.10
  316.6 1.4 fusion.35
  318.0 0.7 copy.15
  (7 shorter events, 0.1 us)
Async XLA Ops:
  7.2 77.1 %all-gather.2.cloned.1.call-start = ((), (), s32[]{:S(2)}) async-start(), calls=%async_computation.1 | async-start | bytes 8912896 | tf_op jit(solution)/shard_map/all_gather | solution.py:133
  7.9 212.4 %reduce-scatter.2.cloned.1.call-start = ((), (), s32[]{:S(2)}) async-start(), calls=%async_computation.2 | async-start | bytes 4718592 | tf_op jit(solution)/shard_map/reduce_scatter | solution.py:135
Sparse Core Ops, SparseCore 0:
  10.1 74.0 all-gather.1
  185.8 34.4 reduce-scatter.1

commit v2 on v1

--- a/solution.py
+++ b/solution.py
@@ -5,25 +5,313 @@
 from jax.experimental.pallas import tpu as pltpu
 from jax.sharding import PartitionSpec as P
 
-N_ROWS = 16
+SIDE = 4
+N_ROWS = SIDE * SIDE
 N_COLS = 8
+TILE = 128
+CAP = 320
+OWN = 8
+PANEL = OWN * N_COLS
+PARTS = 4
+WIDTH = TILE // PARTS
+GROUP = 32
+STAGE = 8
+SLOTS = 8
 MESH = pl.DeviceIdType.MESH
-
-
-def panel_partial(tiles, rows_idx, cols_idx, count, columns, panel_blocks):
-    tile_size = tiles.shape[1]
-    width = columns.shape[1]
-    blocks = columns.reshape(-1, tile_size, width)
-    picked = jnp.take(blocks, cols_idx, axis=0)
-    products = jnp.einsum("cij,cjk->cik", tiles, picked, precision=lax.Precision.HIGHEST)
-    slots = jnp.arange(tiles.shape[0], dtype=jnp.int32)
-    live = slots < count
-    onehot = (
-        (rows_idx[None, :] == jnp.arange(panel_blocks, dtype=jnp.int32)[:, None]) & live[None, :]
-    ).astype(tiles.dtype)
-    return jnp.einsum("pc,cik->pik", onehot, products, precision=lax.Precision.HIGHEST).reshape(
-        -1, width
-    )
+DMA = pltpu.SemaphoreType.DMA
+
+
+def halves(value):
+    high = value.astype(jnp.bfloat16)
+    low = (value - high.astype(jnp.float32)).astype(jnp.bfloat16)
+    return high, low
+
+
+def product_kernel(
+    order, columns, last, keep, tiles, probes, out,
+    own, gx, pairs, stage, xpair, sums, panel, near, mid, far,
+    stage_sem, sa, ra, sb, rb, sc, rc, sd, rd, se, re, sf, rf, sg, rg,
+):
+    r, c = lax.axis_index("rows"), lax.axis_index("cols")
+    y, z = r // SIDE, lax.rem(r, SIDE)
+    x, q = c // 2, lax.rem(c, 2)
+
+    def turn(v, off):
+        return lax.rem(v + off + SIDE, SIDE)
+
+    def yz(dim, off):
+        return (turn(y, off), z) if dim == 0 else (y, turn(z, off))
+
+    def row_peer(dim, off):
+        yy, zz = yz(dim, off)
+        return (yy * SIDE + zz, c)
+
+    def x_peer(off):
+        return (r, turn(x, off) * 2 + q)
+
+    partner = (r, x * 2 + 1 - q)
+
+    def load(i, slot):
+        return pltpu.make_async_copy(tiles.at[pl.ds(i * STAGE, STAGE)], stage.at[slot], stage_sem.at[slot])
+
+    for i in range(SLOTS):
+        load(i, i).start()
+
+    barrier = pltpu.get_barrier_semaphore()
+    peers = [row_peer(dim, off) for dim in (0, 1) for off in (1, -1)] + [x_peer(1), x_peer(-1), partner]
+    for peer in peers:
+        pl.semaphore_signal(barrier, inc=1, device_id=peer, device_id_type=MESH)
+
+    def turned(b, carry):
+        block = jnp.transpose(probes[b])
+        for j in range(PARTS):
+            own[j, b] = block[j * WIDTH:(j + 1) * WIDTH]
+            gx[j, y, z, b] = block[j * WIDTH:(j + 1) * WIDTH]
+        return carry
+
+    lax.fori_loop(0, OWN, turned, 0)
+    pl.semaphore_wait(barrier, len(peers))
+
+    def remote(src, dst, send, recv, to):
+        return pltpu.make_async_remote_copy(
+            src_ref=src, dst_ref=dst, send_sem=send, recv_sem=recv, device_id=to, device_id_type=MESH)
+
+    def step_of(s):
+        return 1 if s == 0 else -1
+
+    def copy_a(j, h, s):
+        return remote(own.at[j, pl.ds(4 * h, 4)], gx.at[j, y, z, pl.ds(4 * h, 4)],
+                      sa.at[j, h, s], ra.at[j, h, s], row_peer(1 - h, step_of(s)))
+
+    def copy_b(j, h, s):
+        yy, zz = yz(1 - h, -step_of(s))
+        ref = gx.at[j, yy, zz, pl.ds(4 * h + 2 * s, 2)]
+        return remote(ref, ref, sb.at[j, h, s], rb.at[j, h, s], row_peer(1 - h, step_of(s)))
+
+    def copy_c(j, h, s):
+        ref = gx.at[j, y, :, pl.ds(4 * h, 4)] if h == 0 else gx.at[j, :, z, pl.ds(4 * h, 4)]
+        return remote(ref, ref, sc.at[j, h, s], rc.at[j, h, s], row_peer(h, step_of(s)))
+
+    def copy_d(j, h, s):
+        yy, zz = yz(h, -step_of(s))
+        cut = pl.ds(4 * h + 2 * s, 2)
+        ref = gx.at[j, yy, :, cut] if h == 0 else gx.at[j, :, zz, cut]
+        return remote(ref, ref, sd.at[j, h, s], rd.at[j, h, s], row_peer(h, step_of(s)))
+
+    ways = [(h, s) for h in (0, 1) for s in (0, 1)]
+
+    def do_a(j):
+        for h, s in ways:
+            copy_a(j, h, s).start()
+
+    def do_b(j):
+        for h, s in ways:
+            copy_a(j, h, s).wait_recv()
+            copy_b(j, h, s).start()
+
+    def do_c(j):
+        for h in (0, 1):
+            copy_b(j, h, 0).wait_recv()
+            copy_b(j, h, 1).wait_recv()
+            copy_c(j, h, 0).start()
+            copy_c(j, h, 1).start()
+
+    def do_d(j):
+        for h, s in ways:
+            copy_c(j, h, s).wait_recv()
+            copy_d(j, h, s).start()
+
+    def do_e(j):
+        for h, s in ways:
+            copy_d(j, h, s).wait_recv()
+
+    def split(i, carry):
+        slot = lax.rem(i, SLOTS)
+        load(i, slot).wait()
+        for k in range(STAGE):
+            high, low = halves(jnp.transpose(stage[slot, k]))
+            pairs[i * STAGE + k, 0:TILE] = high
+            pairs[i * STAGE + k, TILE:2 * TILE] = low
+
+        @pl.when(i + SLOTS < CAP // STAGE)
+        def _():
+            load(i + SLOTS, slot).start()
+
+        return carry
+
+    def spread(j):
+        def one(g, carry):
+            high, low = halves(gx[j, g // 32, lax.rem(g // 8, 4), lax.rem(g, 8)])
+            xpair[g, 0:WIDTH, 0:TILE] = high
+            xpair[g, 0:WIDTH, TILE:2 * TILE] = high
+            xpair[g, WIDTH:2 * WIDTH, 0:TILE] = low
+            xpair[g, WIDTH:2 * WIDTH, TILE:2 * TILE] = low
+            return carry
+
+        lax.fori_loop(0, N_ROWS * OWN, one, 0, unroll=8)
+
+    def multiply(first, count, run):
+        def group(g, run):
+            for u in range(GROUP):
+                t = first + g * GROUP + u
+                both = jnp.dot(xpair[columns[t]], pairs[order[t]], preferred_element_type=jnp.float32)
+                run = run * keep[t] + (both[:WIDTH] + both[WIDTH:])
+                sums[t] = run
+            return run
+
+        return lax.fori_loop(0, count // GROUP, group, run)
+
+    def collect(j):
+        def one(i, carry):
+            at = last[i]
+            panel[j, i // 16, lax.rem(i // 8, 2), lax.rem(i, 8)] = jnp.where(
+                at >= 0, sums[jnp.maximum(at, 0)], 0.0)
+            return carry
+
+        lax.fori_loop(0, PANEL, one, 0, unroll=8)
+
+    def swap(j):
+        return remote(panel.at[j, :, 1 - q], near.at[j], se.at[j], re.at[j], partner)
+
+    def copy_f(j, s):
+        return remote(panel.at[j, turn(x, 2), q, pl.ds(4 * s, 4)], mid.at[j, s],
+                      sf.at[j, s], rf.at[j, s], x_peer(step_of(s)))
+
+    def copy_g(j, s):
+        return remote(panel.at[j, turn(x, step_of(s)), q], far.at[j, s],
+                      sg.at[j, s], rg.at[j, s], x_peer(step_of(s)))
+
+    def do_p(j):
+        collect(j)
+        swap(j).start()
+
+    def do_q(j):
+        swap(j).wait_recv()
+        for off in (2, 1, -1, 0):
+            at = turn(x, off)
+            panel[j, at, q] = panel[j, at, q] + near[j, at]
+            if off == 2:
+                copy_f(j, 0).start()
+                copy_f(j, 1).start()
+
+    def do_r(j):
+        for s in (0, 1):
+            copy_f(j, s).wait_recv()
+            at = turn(x, step_of(s))
+            cut = pl.ds(4 * s, 4)
+            panel[j, at, q, cut] = panel[j, at, q, cut] + mid[j, s]
+            copy_g(j, s).start()
+
+    def do_s(j):
+        copy_g(j, 0).wait_recv()
+        copy_g(j, 1).wait_recv()
+        out[:, j * WIDTH:(j + 1) * WIDTH, :] = panel[j, x, q] + (far[j, 0] + far[j, 1])
+
+    steps = CAP // STAGE
+
+    def some(lo, hi):
+        lax.fori_loop(lo, hi, split, 0)
+
+    for j in range(PARTS):
+        do_a(j)
+    some(0, 5)
+    do_b(0)
+    some(5, 8)
+    do_b(1)
+    some(8, 11)
+    do_b(2)
+    do_c(0)
+    some(11, 15)
+    do_b(3)
+    do_c(1)
+    some(15, 28)
+    do_d(0)
+    do_c(2)
+    some(28, steps)
+    do_e(0)
+
+    zero = jnp.zeros((WIDTH, TILE), jnp.float32)
+    cuts = (0, 64, 160, 224, 320)
+
+    def part(j, between):
+        spread(j)
+        run = zero
+        for k in range(4):
+            run = multiply(cuts[k], cuts[k + 1] - cuts[k], run)
+            for act, i in between[k]:
+                act(i)
+
+    part(0, [[(do_d, 1), (do_c, 3)], [], [], [(do_p, 0)]])
+    do_e(1)
+    part(1, [[(do_q, 0)], [(do_d, 2)], [], [(do_r, 0), (do_p, 1)]])
+    do_e(2)
+    part(2, [[(do_d, 3)], [(do_q, 1), (do_s, 0)], [], [(do_r, 1), (do_p, 2)]])
+    do_e(3)
+    part(3, [[], [(do_q, 2), (do_s, 1)], [], [(do_r, 2), (do_p, 3)]])
+    do_q(3)
+    do_s(2)
+    do_r(3)
+    do_s(3)
+    for j in range(PARTS):
+        for h, s in ways:
+            for copy in (copy_a, copy_b, copy_c, copy_d):
+                copy(j, h, s).wait_send()
+        swap(j).wait_send()
+        for s in (0, 1):
+            copy_f(j, s).wait_send()
+            copy_g(j, s).wait_send()
+
+
+def sorted_slots(rows_idx, cols_idx, count):
+    slots = jnp.arange(CAP, dtype=jnp.int32)
+    key = jnp.where(slots < count, rows_idx, PANEL) * CAP + slots
+    rank = jnp.sum((key[None, :] < key[:, None]).astype(jnp.int32), axis=1)
+    chosen = rank[None, :] == slots[:, None]
+
+    def pick(values):
+        return jnp.sum(jnp.where(chosen, values[None, :], 0), axis=1)
+
+    order = pick(slots)
+    columns = pick(cols_idx)
+    row = pick(key) // CAP
+    keep = jnp.concatenate([jnp.zeros((1,), jnp.float32), (row[1:] == row[:-1]).astype(jnp.float32)])
+    panels = jnp.arange(PANEL, dtype=jnp.int32)
+    here = row[None, :] == panels[:, None]
+    last = jnp.max(jnp.where(here, slots[None, :], -1), axis=1)
+    return order, columns, last, keep
+
+
+def product(tiles, rows_idx, cols_idx, count, probes):
+    order, columns, last, keep = sorted_slots(rows_idx, cols_idx, count)
+    scalar = pl.BlockSpec(memory_space=pltpu.SMEM)
+    vector = pl.BlockSpec(memory_space=pltpu.VMEM)
+    f32, bf16 = jnp.float32, jnp.bfloat16
+    piece = (OWN, WIDTH, TILE)
+    return pl.pallas_call(
+        product_kernel,
+        out_shape=jax.ShapeDtypeStruct((OWN, TILE, TILE), f32),
+        in_specs=[scalar] * 4 + [pl.BlockSpec(memory_space=pl.ANY), vector],
+        out_specs=vector,
+        scratch_shapes=[
+            pltpu.VMEM((PARTS,) + piece, f32),
+            pltpu.VMEM((PARTS, SIDE, SIDE) + piece, f32),
+            pltpu.VMEM((CAP, 2 * TILE, TILE), bf16),
+            pltpu.VMEM((SLOTS, STAGE, TILE, TILE), f32),
+            pltpu.VMEM((N_ROWS * OWN, 2 * WIDTH, 2 * TILE), bf16),
+            pltpu.VMEM((CAP, WIDTH, TILE), f32),
+            pltpu.VMEM((PARTS, SIDE, 2) + piece, f32),
+            pltpu.VMEM((PARTS, SIDE) + piece, f32),
+            pltpu.VMEM((PARTS, 2, OWN // 2, WIDTH, TILE), f32),
+            pltpu.VMEM((PARTS, 2) + piece, f32),
+            DMA((SLOTS,)),
+        ]
+        + [DMA((PARTS, 2, 2))] * 8
+        + [DMA((PARTS,))] * 2
+        + [DMA((PARTS, 2))] * 4,
+        compiler_params=pltpu.CompilerParams(
+            collective_id=2, has_side_effects=True, vmem_limit_bytes=60 * 2**20),
+        name="product",
+    )(order, columns, last, keep, tiles, probes.reshape(OWN, TILE, TILE))
 
 
 def local_gram(matrix):
@@ -127,12 +415,9 @@
     cols_idx = tile_cols[0, 0]
     count = tile_count[0, 0]
     own_rows = probes.shape[0]
-    tile_size = tiles.shape[1]
     nodes = own_rows * N_ROWS * N_COLS
-    panel_blocks = N_COLS * own_rows // tile_size
-    gathered = lax.all_gather(probes, "rows", axis=0, tiled=True)
-    panel = panel_partial(tiles, rows_idx, cols_idx, count, gathered, panel_blocks)
-    own = lax.psum_scatter(panel, "cols", scatter_dimension=0, tiled=True)
+    blocks = product(tiles, rows_idx, cols_idx, count, probes)
+    own = jnp.swapaxes(blocks, 1, 2).reshape(own_rows, TILE)
     gram = sum_everywhere(local_gram(own), 1)
     lower, inverse = triangle_inverse(gram, nodes)
     first = jnp.dot(own, inverse.T, precision=lax.Precision.HIGHEST)

time: 326 us -> 182 us (0.56)
  waiting for transfers between devices: 109 us -> 0 us
  Pallas kernels: 39.8 us -> 118 us
  matrix products: 68.7 us -> 7.7 us
  local copies, waits for them, and re-layouts: 43.9 us -> 2.34 us
  between operations: 14.8 us -> 1.42 us
    pallas_call x0 -> x1, Pallas kernels: none -> 82.8 us  [product(): pl.pallas_call(product_kernel, out_shape=jax.ShapeDtypeStruct((OWN, TILE,...]
    all_gather x1 -> x0, waiting for transfers between devices: 73.5 us -> none  [shards(): gathered = lax.all_gather(probes, 'rows', axis=0, tiled=True)]
    dot_general x2 -> x0, matrix products: 58.4 us -> none  [the longest x1 45 us: panel_partial(): jnp.einsum('cij,cjk->cik', tiles, picked, precision=lax.Precision.HIGHEST)]
    reduce_scatter x1 -> x0, waiting for transfers between devices: 34.6 us -> none  [shards(): own = lax.psum_scatter(panel, 'cols', scatter_dimension=0, tiled=True)]
    dot_general x2 -> x1, local copies, waits for them, and re-layouts: 25.8 us -> 0.2 us  [local_gram(): jnp.einsum('rk,rl->kl', matrix, matrix, precision=lax.Precision.HIGHEST)]
    gather x1 -> x0, local copies, waits for them, and re-layouts: 17.2 us -> none  [panel_partial(): picked = jnp.take(blocks, cols_idx, axis=0)]
    pallas_call x2, Pallas kernels: 39.8 us -> 35.4 us  [sum_everywhere(): pl.pallas_call(sum_kernel, out_shape=jax.ShapeDtypeStruct((N_COLS,) + pie...]
  transfers between devices with their start and end apart: 2 -> 0, of which waited for: 2 -> 0; matrix products, arithmetic and copies ran while one was open for 1% -> 0% of each run, Pallas kernels for 0% -> 0%
where the time goes in v2:
time: 182 us; the launch traced here: 181 us
  Pallas kernels  118 us (65%)
  other arithmetic  51.5 us (28%)
  matrix products  7.7 us (4%)
  local copies, waits for them, and re-layouts  2.34 us (1%)
    pallas_call x1, Pallas kernels, product(): pl.pallas_call(product_kernel, out_shape=jax.ShapeDtypeStruct((OWN, TILE,...  82.8 us
    pallas_call x2, Pallas kernels, sum_everywhere(): pl.pallas_call(sum_kernel, out_shape=jax.ShapeDtypeStruct((N_COLS,) + pie...  35.4 us
    another operation x6, other arithmetic, triangle_inverse(): lower = jnp.linalg.cholesky(gram / nodes)  24.9 us
    another operation x3, other arithmetic, triangle_inverse(): jax.scipy.linalg.solve_triangular(lower, jnp.eye(gram.shape[0], dtype=gra...  20.3 us

profile of v2, /device:TPU:1, one launch (start us, length us, event | category | flops | bytes accessed | tf_op | source)
XLA Modules:
  0.0 181.2 jit_solution(10294776246222948759)
XLA Ops:
  1.3 0.7 reduce.4
  2.0 0.2 convert_reduce_fusion
  2.2 0.7 reduce.5
  2.9 0.9 select_reduce_fusion
  3.8 0.1 slice_compare_fusion
  3.9 0.7 select_reduce_fusion.3.last
  4.6 0.7 add_convert_fusion.keep
  5.3 82.8 %product.1 = f32[8,128,128]{2,1,0:T(8,128)} custom-call(s32[320]{0:T(512)} %get-tuple-element.19.order, s32[320]{0:T(512)} %get-tuple-element.18.columns, s32[64]{0:T(128)} %select_reduce_fusion.3.last, f32[320]{0:T(512)} %add_convert_fusion.keep, f32[320,128,128]{2,1,0:T(8,128)} %bitcast.44, f32[8,128,128]{2,1,0:T(8,128)} %bitcast.52), custom_call_target="tpu_custom_call" | custom-call | tf_op jit(solution)/shard_map/product/pallas_call | solution.py:290
  88.1 1.2 copy.23
  89.3 0.2 copy.24
  89.5 1.3 fusion.19.g_ref
  90.8 18.1 %sum_everywhere.2 = f32[8,16,128]{2,1,0:T(8,128)} custom-call(f32[8,16,128]{2,1,0:T(8,128)} %fusion.19.g_ref), custom_call_target="tpu_custom_call" | custom-call | tf_op jit(solution)/shard_map/sum_everywhere/pallas_call | solution.py:395
  108.9 0.8 broadcast_multiply_fusion.1
  109.8 0.1 copy.25
  109.9 11.7 %cholesky.44 = f32[128,128]{1,0:T(8,128)S(1)} custom-call(f32[128,128]{1,0:T(8,128)S(1)} %fusion.7), custom_call_target="Cholesky" | custom-call | tf_op jit(solution)/shard_map/jit(cholesky)/cholesky | solution.py:322
  121.6 0.6 compare_reduce_fusion.1
  122.3 0.7 fusion.10
  122.9 0.7 copy.27
  123.7 9.8 %custom-call.6 = f32[1,128,128]{1,2,0:T(8,128)S(1)} custom-call(f32[1,128,128]{2,1,0:T(8,128)S(1)} %get-tuple-element.21), custom_call_target="InvertDiagBlocksLowerTriangular" | custom-call | tf_op jit(solution)/shard_map/jit(_solve_triangular)/triangular_solve | solution.py:323
  133.5 0.3 fusion.2
  133.8 0.6 fusion.20
  134.3 1.6 fusion.21
  136.0 17.3 %sum_everywhere.3 = f32[8,16,128]{2,1,0:T(8,128)} custom-call(f32[8,16,128]{2,1,0:T(8,128)} %bitcast.53), custom_call_target="tpu_custom_call" | custom-call | tf_op jit(solution)/shard_map/sum_everywhere/pallas_call | solution.py:395
  153.3 0.8 broadcast_multiply_fusion
  154.1 0.1 copy.26
  154.2 11.7 %cholesky.55 = f32[128,128]{1,0:T(8,128)S(1)} custom-call(f32[128,128]{1,0:T(8,128)S(1)} %fusion.5), custom_call_target="Cholesky" | custom-call | tf_op jit(solution)/shard_map/jit(cholesky)/cholesky | solution.py:322
  166.0 0.7 compare_reduce_fusion
  166.7 2.3 %fusion.9 = f32[128,128]{1,0:T(8,128)} fusion(f32[128,128]{1,0:T(8,128)S(1)} %cholesky.55, f32[128,128]{1,0:T(8,128)S(1)} %cholesky.44, pred[]{:T(512)} %compare_reduce_fusion, pred[]{:T(512)} %compare_reduce_fusion.1), kind=kOutput, calls=%fused_computation.25 | convolution fusion | flops 25264128 | bytes 196610 | tf_op jit(solution)/shard_map/dot_general | solution.py:427
  169.0 0.7 select_bitcast_fusion
  169.7 9.8 %custom-call.7 = f32[1,128,128]{1,2,0:T(8,128)S(1)} custom-call(f32[1,128,128]{2,1,0:T(8,128)S(1)} %select_bitcast_fusion), custom_call_target="InvertDiagBlocksLowerTriangular" | custom-call | tf_op jit(solution)/shard_map/jit(_solve_triangular)/triangular_solve | solution.py:323
  179.5 0.3 fusion
  179.8 1.4 fusion.22
  (6 shorter events, 0.1 us)

commit v3 on v2

v3 whole, which is shorter than its diff:
```python
import jax
import jax.numpy as jnp
from jax import lax
from jax.experimental import pallas as pl
from jax.experimental.pallas import tpu as pltpu
from jax.sharding import PartitionSpec as P

SIDE = 4
N_ROWS = SIDE * SIDE
N_COLS = 8
TILE = 128
CAP = 320
OWN = 8
PANEL = OWN * N_COLS
PARTS = 4
WIDTH = TILE // PARTS
GROUP = 32
STAGE = 8
STRIP = 16
SLICE = TILE // N_COLS
NODES = OWN * TILE * N_ROWS * N_COLS
SLOTS = 8
MESH = pl.DeviceIdType.MESH
DMA = pltpu.SemaphoreType.DMA


def halves(value):
    high = value.astype(jnp.bfloat16)
    low = (value - high.astype(jnp.float32)).astype(jnp.bfloat16)
    return high, low


def exact(left, right, at, to):
    return lax.dot_general(
        left, right, (((at,), (to,)), ((), ())), precision=lax.Precision.HIGHEST,
        preferred_element_type=jnp.float32)


def triangles(gram, upper, inverse, work):
    rows = lax.broadcasted_iota(jnp.int32, (TILE, TILE), 0)
    cols = lax.broadcasted_iota(jnp.int32, (TILE, TILE), 1)
    work[:, 0:TILE] = gram
    work[:, TILE:2 * TILE] = jnp.where(rows == cols, 1.0, 0.0)
    shape = (STRIP, TILE)
    place = lax.broadcasted_iota(jnp.int32, shape, 0)
    for lo in range(0, TILE, STRIP):
        hi = lo + STRIP
        strip = work[lo:hi, 0:TILE]
        turned = work[lo:hi, TILE:2 * TILE]
        columns = [jnp.broadcast_to(strip[:, lo + j:lo + j + 1], shape) for j in range(STRIP)]
        for k in range(STRIP):
            scale = lax.rsqrt(jnp.broadcast_to(columns[k][k:k + 1], shape))
            weight = columns[k] * scale
            for j in range(k + 1, STRIP):
                columns[j] = columns[j] - weight * jnp.broadcast_to(weight[j:j + 1], shape)
            pivot = jnp.broadcast_to(strip[k:k + 1], shape) * scale
            other = jnp.broadcast_to(turned[k:k + 1], shape) * scale
            weight = jnp.where(place > k, weight, 0.0)
            strip = jnp.where(place == k, pivot, strip - weight * pivot)
            turned = jnp.where(place == k, other, turned - weight * other)
        strip = jnp.where(cols[lo:hi] >= rows[lo:hi], strip, 0.0)
        upper[lo:hi, :] = strip
        inverse[lo:hi, :] = turned
        if hi < TILE:
            change = exact(strip, jnp.concatenate([strip, turned], axis=1), 0, 0)
            work[hi:, :] = work[hi:, :] - change[hi:, :]


def sort_slots(count, rows_idx, cols_idx, plan):
    blocks = CAP // TILE + 1
    square = (TILE, TILE)
    lane = lax.broadcasted_iota(jnp.int32, (1, TILE), 1)
    high = lax.broadcasted_iota(jnp.int32, square, 0)
    wide = lax.broadcasted_iota(jnp.int32, square, 1)

    def block(ref, b):
        width = min(TILE, CAP - b * TILE)
        value = ref[:, b * TILE:b * TILE + width]
        if width < TILE:
            value = jnp.concatenate([value, jnp.zeros((1, TILE - width), jnp.int32)], axis=1)
        return value

    def down(value):
        return jnp.transpose(jnp.broadcast_to(value, square))

    def total(mask, value=1):
        return jnp.sum(jnp.where(mask, value, 0), axis=0, keepdims=True)

    slot = [lane + b * TILE for b in range(blocks)]
    row = [jnp.where(slot[b] < count, block(rows_idx, b), PANEL) for b in range(blocks)]
    row_down = [down(v) for v in row]
    place, packed = [], []
    for b in range(blocks):
        rank = jnp.zeros((1, TILE), jnp.int32)
        before = jnp.zeros((1, TILE), jnp.int32)
        for a in range(blocks):
            same = row_down[a] == row[b]
            if a == b:
                same = jnp.logical_and(same, high < wide)
            earlier = row_down[a] < row[b]
            if a <= b:
                earlier = jnp.logical_or(earlier, same)
                before = before + total(same)
            rank = rank + total(earlier)
        place.append(down(rank))
        goes_on = jnp.where(before > 0, 1, 0)
        packed.append(down((goes_on * blocks * TILE + slot[b]) * TILE + block(cols_idx, b)))
    for b in range(blocks):
        value = jnp.zeros((1, TILE), jnp.int32)
        for a in range(blocks):
            value = value + total(place[a] == wide + b * TILE, packed[a])
        rest = value // TILE
        cut = pl.ds(b * TILE, TILE)
        plan[0:1, cut] = rest % (blocks * TILE)
        plan[1:2, cut] = value % TILE
        plan[2:3, cut] = rest // (blocks * TILE)
        upto = jnp.zeros((1, TILE), jnp.int32)
        here = jnp.zeros((1, TILE), jnp.int32)
        for a in range(blocks):
            upto = upto + total(row_down[a] <= wide)
            here = here + total(row_down[a] == wide)
        plan[3:4, cut] = jnp.where(here > 0, upto - 1, -1)


def product_kernel(
    count, rows_idx, cols_idx, tiles, probes, basis, factor, first_factor,
    own, gx, pairs, stage, xpair, sums, panel, near, mid, far,
    plan, table, mats, share, slices, grams, got_cols, got_rows, work, uppers, lowers,
    stage_sem, sa, ra, sb, rb, sc, rc, sd, rd, se, re, sf, rf, sg, rg,
    table_sem, sh, rh, si, ri, sj, rj,
):
    r, c = lax.axis_index("rows"), lax.axis_index("cols")
    y, z = r // SIDE, lax.rem(r, SIDE)
    x, q = c // 2, lax.rem(c, 2)

    def turn(v, off):
        return lax.rem(v + off + SIDE, SIDE)

    def yz(dim, off):
        return (turn(y, off), z) if dim == 0 else (y, turn(z, off))

    def row_peer(dim, off):
        yy, zz = yz(dim, off)
        return (yy * SIDE + zz, c)

    def x_peer(off):
        return (r, turn(x, off) * 2 + q)

    partner = (r, x * 2 + 1 - q)

    def load(i, slot):
        return pltpu.make_async_copy(tiles.at[pl.ds(i * STAGE, STAGE)], stage.at[slot], stage_sem.at[slot])

    for i in range(SLOTS):
        load(i, i).start()

    barrier = pltpu.get_barrier_semaphore()

    def col_mate(d):
        return (r, lax.rem(c + d, N_COLS))

    def row_mate(d):
        return (lax.rem(r + d, N_ROWS), c)

    for d in range(1, N_COLS):
        pl.semaphore_signal(barrier, inc=1, device_id=col_mate(d), device_id_type=MESH)
    for d in range(1, N_ROWS):
        pl.semaphore_signal(barrier, inc=1, device_id=row_mate(d), device_id_type=MESH)

    def turned(b, carry):
        block = jnp.transpose(probes[b])
        for j in range(PARTS):
            own[j, b] = block[j * WIDTH:(j + 1) * WIDTH]
            gx[j, y, z, b] = block[j * WIDTH:(j + 1) * WIDTH]
        return carry

    lax.fori_loop(0, OWN, turned, 0)
    pl.semaphore_wait(barrier, N_COLS - 1 + N_ROWS - 1)

    def remote(src, dst, send, recv, to):
        return pltpu.make_async_remote_copy(
            src_ref=src, dst_ref=dst, send_sem=send, recv_sem=recv, device_id=to, device_id_type=MESH)

    def step_of(s):
        return 1 if s == 0 else -1

    def copy_a(j, h, s):
        return remote(own.at[j, pl.ds(4 * h, 4)], gx.at[j, y, z, pl.ds(4 * h, 4)],
                      sa.at[j, h, s], ra.at[j, h, s], row_peer(1 - h, step_of(s)))

    def copy_b(j, h, s):
        yy, zz = yz(1 - h, -step_of(s))
        ref = gx.at[j, yy, zz, pl.ds(4 * h + 2 * s, 2)]
        return remote(ref, ref, sb.at[j, h, s], rb.at[j, h, s], row_peer(1 - h, step_of(s)))

    def copy_c(j, h, s):
        ref = gx.at[j, y, :, pl.ds(4 * h, 4)] if h == 0 else gx.at[j, :, z, pl.ds(4 * h, 4)]
        return remote(ref, ref, sc.at[j, h, s], rc.at[j, h, s], row_peer(h, step_of(s)))

    def copy_d(j, h, s):
        yy, zz = yz(h, -step_of(s))
        cut = pl.ds(4 * h + 2 * s, 2)
        ref = gx.at[j, yy, :, cut] if h == 0 else gx.at[j, :, zz, cut]
        return remote(ref, ref, sd.at[j, h, s], rd.at[j, h, s], row_peer(h, step_of(s)))

    ways = [(h, s) for h in (0, 1) for s in (0, 1)]

    def do_a(j):
        for h, s in ways:
            copy_a(j, h, s).start()

    def do_b(j):
        for h, s in ways:
            copy_a(j, h, s).wait_recv()
            copy_b(j, h, s).start()

    def do_c(j):
        for h in (0, 1):
            copy_b(j, h, 0).wait_recv()
            copy_b(j, h, 1).wait_recv()
            copy_c(j, h, 0).start()
            copy_c(j, h, 1).start()

    def do_d(j):
        for h, s in ways:
            copy_c(j, h, s).wait_recv()
            copy_d(j, h, s).start()

    def do_e(j):
        for h, s in ways:
            copy_d(j, h, s).wait_recv()

    def split(i, carry):
        slot = lax.rem(i, SLOTS)
        load(i, slot).wait()
        for k in range(STAGE):
            high, low = halves(jnp.transpose(stage[slot, k]))
            pairs[i * STAGE + k, 0:TILE] = high
            pairs[i * STAGE + k, TILE:2 * TILE] = low

        @pl.when(i + SLOTS < CAP // STAGE)
        def _():
            load(i + SLOTS, slot).start()

        return carry

    def spread(j):
        def one(g, carry):
            high, low = halves(gx[j, g // 32, lax.rem(g // 8, 4), lax.rem(g, 8)])
            xpair[g, 0:WIDTH, 0:TILE] = high
            xpair[g, 0:WIDTH, TILE:2 * TILE] = high
            xpair[g, WIDTH:2 * WIDTH, 0:TILE] = low
            xpair[g, WIDTH:2 * WIDTH, TILE:2 * TILE] = low
            return carry

        lax.fori_loop(0, N_ROWS * OWN, one, 0, unroll=8)

    def multiply(first, count, run):
        def group(g, run):
            for u in range(GROUP):
                t = first + g * GROUP + u
                both = jnp.dot(xpair[table[1, t]], pairs[table[0, t]], preferred_element_type=jnp.float32)
                run = run * table[2, t].astype(jnp.float32) + (both[:WIDTH] + both[WIDTH:])
                sums[t] = run
            return run

        return lax.fori_loop(0, count // GROUP, group, run)

    def collect(j):
        def one(i, carry):
            at = table[3, i]
            panel[j, i // 16, lax.rem(i // 8, 2), lax.rem(i, 8)] = jnp.where(
                at >= 0, sums[jnp.maximum(at, 0)], 0.0)
            return carry

        lax.fori_loop(0, PANEL, one, 0, unroll=8)

    def swap(j):
        return remote(panel.at[j, :, 1 - q], near.at[j], se.at[j], re.at[j], partner)

    def copy_f(j, s):
        return remote(panel.at[j, turn(x, 2), q, pl.ds(4 * s, 4)], mid.at[j, s],
                      sf.at[j, s], rf.at[j, s], x_peer(step_of(s)))

    def copy_g(j, s):
        return remote(panel.at[j, turn(x, step_of(s)), q], far.at[j, s],
                      sg.at[j, s], rg.at[j, s], x_peer(step_of(s)))

    def do_p(j):
        collect(j)
        swap(j).start()

    def do_q(j):
        swap(j).wait_recv()
        for off in (2, 1, -1, 0):
            at = turn(x, off)
            panel[j, at, q] = panel[j, at, q] + near[j, at]
            if off == 2:
                copy_f(j, 0).start()
                copy_f(j, 1).start()

    def do_r(j):
        for s in (0, 1):
            copy_f(j, s).wait_recv()
            at = turn(x, step_of(s))
            cut = pl.ds(4 * s, 4)
            panel[j, at, q, cut] = panel[j, at, q, cut] + mid[j, s]
            copy_g(j, s).start()

    def do_s(j):
        copy_g(j, 0).wait_recv()
        copy_g(j, 1).wait_recv()
        mats[0, :, j * WIDTH:(j + 1) * WIDTH, :] = panel[j, x, q] + (far[j, 0] + far[j, 1])

    steps = CAP // STAGE

    def some(lo, hi):
        lax.fori_loop(lo, hi, split, 0)

    for j in range(PARTS):
        do_a(j)
    sort_slots(count[0, 0], rows_idx, cols_idx, plan)
    to_scalars = pltpu.make_async_copy(plan, table, table_sem)
    to_scalars.start()
    some(0, 3)
    do_b(0)
    some(3, 6)
    do_b(1)
    some(6, 9)
    do_b(2)
    do_c(0)
    some(9, 14)
    do_b(3)
    do_c(1)
    some(14, 26)
    do_d(0)
    do_c(2)
    some(26, steps)
    to_scalars.wait()
    do_e(0)

    zero = jnp.zeros((WIDTH, TILE), jnp.float32)
    cuts = (0, 64, 160, 224, 320)

    def part(j, between):
        spread(j)
        run = zero
        for k in range(4):
            run = multiply(cuts[k], cuts[k + 1] - cuts[k], run)
            for act, i in between[k]:
                act(i)

    part(0, [[(do_d, 1), (do_c, 3)], [], [], [(do_p, 0)]])
    do_e(1)
    part(1, [[(do_q, 0)], [(do_d, 2)], [], [(do_r, 0), (do_p, 1)]])
    do_e(2)
    part(2, [[(do_d, 3)], [(do_q, 1), (do_s, 0)], [], [(do_r, 1), (do_p, 2)]])
    do_e(3)
    part(3, [[], [(do_q, 2), (do_s, 1)], [], [(do_r, 2), (do_p, 3)]])
    do_q(3)
    do_s(2)
    do_r(3)
    do_s(3)

    def copy_h(p, d):
        to = lax.rem(c + d, N_COLS)
        return remote(share.at[p, to], got_cols.at[p, d], sh.at[p, d], rh.at[p, d], col_mate(d))

    def copy_i(p, d):
        return remote(slices.at[p], got_rows.at[p, r], si.at[p, d], ri.at[p, d], row_mate(d))

    def copy_j(p, d):
        return remote(grams.at[p, c], grams.at[p, c], sj.at[p, d], rj.at[p, d], col_mate(d))

    def orthogonal(p, carry):
        total = jnp.zeros((TILE, TILE), jnp.float32)
        for b in range(OWN):
            block = mats[p, b]
            total = total + exact(block, block, 1, 1)
        share[p] = total.reshape(N_COLS, SLICE, TILE)
        for d in range(1, N_COLS):
            copy_h(p, d).start()
        for d in range(1, N_COLS):
            copy_h(p, d).wait_recv()
        part = share[p, c]
        for d in range(1, N_COLS):
            part = part + got_cols[p, d]
        slices[p] = part
        got_rows[p, r] = part
        for d in range(1, N_ROWS):
            copy_i(p, d).start()
        for d in range(1, N_ROWS):
            copy_i(p, d).wait_recv()
        part = got_rows[p, 0]
        for d in range(1, N_ROWS):
            part = part + got_rows[p, d]
        grams[p, c] = part
        for d in range(1, N_COLS):
            copy_j(p, d).start()
        for d in range(1, N_COLS):
            copy_j(p, d).wait_recv()
        triangles(grams[p].reshape(TILE, TILE) / NODES, uppers.at[p], lowers.at[p], work)
        lower = lowers[p]
        for b in range(OWN):
            mats[p + 1, b] = exact(lower, mats[p, b], 1, 0)
        for d in range(1, N_COLS):
            copy_h(p, d).wait_send()
            copy_j(p, d).wait_send()
        for d in range(1, N_ROWS):
            copy_i(p, d).wait_send()
        return carry

    lax.fori_loop(0, 2, orthogonal, 0)
    for b in range(OWN):
        basis[b] = jnp.transpose(mats[2, b])
    first_factor[...] = uppers[0]
    factor[...] = exact(uppers[1], uppers[0], 1, 0)
    for j in range(PARTS):
        for h, s in ways:
            for copy in (copy_a, copy_b, copy_c, copy_d):
                copy(j, h, s).wait_send()
        swap(j).wait_send()
        for s in (0, 1):
            copy_f(j, s).wait_send()
            copy_g(j, s).wait_send()


def product(tiles, rows_idx, cols_idx, count, probes):
    scalar = pl.BlockSpec(memory_space=pltpu.SMEM)
    vector = pl.BlockSpec(memory_space=pltpu.VMEM)
    f32, bf16 = jnp.float32, jnp.bfloat16
    piece = (OWN, WIDTH, TILE)
    square = (TILE, TILE)
    slab = (SLICE, TILE)
    return pl.pallas_call(
        product_kernel,
        out_shape=[
            jax.ShapeDtypeStruct((OWN,) + square, f32),
            jax.ShapeDtypeStruct(square, f32),
            jax.ShapeDtypeStruct(square, f32),
        ],
        in_specs=[scalar, vector, vector, pl.BlockSpec(memory_space=pl.ANY), vector],
        out_specs=[vector] * 3,
        scratch_shapes=[
            pltpu.VMEM((PARTS,) + piece, f32),
            pltpu.VMEM((PARTS, SIDE, SIDE) + piece, f32),
            pltpu.VMEM((CAP, 2 * TILE, TILE), bf16),
            pltpu.VMEM((SLOTS, STAGE, TILE, TILE), f32),
            pltpu.VMEM((N_ROWS * OWN, 2 * WIDTH, 2 * TILE), bf16),
            pltpu.VMEM((CAP, WIDTH, TILE), f32),
            pltpu.VMEM((PARTS, SIDE, 2) + piece, f32),
            pltpu.VMEM((PARTS, SIDE) + piece, f32),
            pltpu.VMEM((PARTS, 2, OWN // 2, WIDTH, TILE), f32),
            pltpu.VMEM((PARTS, 2) + piece, f32),
            pltpu.VMEM((8, 3 * TILE), jnp.int32),
            pltpu.SMEM((8, 3 * TILE), jnp.int32),
            pltpu.VMEM((3, OWN) + square, f32),
            pltpu.VMEM((2, N_COLS) + slab, f32),
            pltpu.VMEM((2,) + slab, f32),
            pltpu.VMEM((2, N_COLS) + slab, f32),
            pltpu.VMEM((2, N_COLS) + slab, f32),
            pltpu.VMEM((2, N_ROWS) + slab, f32),
            pltpu.VMEM((TILE, 2 * TILE), f32),
            pltpu.VMEM((2,) + square, f32),
            pltpu.VMEM((2,) + square, f32),
            DMA((SLOTS,)),
        ]
        + [DMA((PARTS, 2, 2))] * 8
        + [DMA((PARTS,))] * 2
        + [DMA((PARTS, 2))] * 4
        + [DMA(())]
        + [DMA((2, N_COLS))] * 2
        + [DMA((2, N_ROWS))] * 2
        + [DMA((2, N_COLS))] * 2,
        compiler_params=pltpu.CompilerParams(
            collective_id=2, has_side_effects=True, vmem_limit_bytes=60 * 2**20),
        name="node_basis",
    )(count, rows_idx, cols_idx, tiles, probes.reshape((OWN,) + square))


def shards(tile_values, tile_rows, tile_cols, tile_count, probes):
    basis, factor, first_factor = product(
        tile_values[0, 0], tile_rows[0], tile_cols[0], tile_count, probes)
    return basis.reshape(probes.shape), factor, first_factor


def solution(mesh):
    placed = (
        P("rows", "cols", None, None, None),
        P("rows", "cols", None),
        P("rows", "cols", None),
        P("rows", "cols"),
        P(("rows", "cols"), None),
    )
    return jax.shard_map(
        shards,
        mesh=mesh,
        in_specs=placed,
        out_specs=(P(("rows", "cols"), None), P(), P()),
        check_vma=False,
    )
```

time: 182 us -> 132 us (0.73)
  other arithmetic: 51.5 us -> 0 us
  Pallas kernels: 118 us -> 126 us
  matrix products: 7.7 us -> 0 us
  local copies, waits for them, and re-layouts: 2.34 us -> 4.81 us
    another operation x9 -> x0, other arithmetic: 45.2 us -> none  [the longest x6 24.9 us: triangle_inverse(): lower = jnp.linalg.cholesky(gram / nodes)]
    pallas_call x3 -> x1, Pallas kernels: 118 us -> 126 us  [product(): pl.pallas_call(product_kernel, out_shape=[jax.ShapeDtypeStruct((OWN,) + s...]
    dot_general x5 -> x0, matrix products: 7.13 us -> none  [the longest x2 2.92 us: local_gram(): jnp.einsum('rk,rl->kl', matrix, matrix, precision=lax.Precision.HIGHEST)]
    unnamed x1 -> x3, local copies, waits for them, and re-layouts: 0.73 us -> 4.81 us
where the time goes in v3:
time: 132 us
  Pallas kernels  126 us (95%)
  local copies, waits for them, and re-layouts  4.81 us (4%)
    pallas_call x1, Pallas kernels, product(): pl.pallas_call(product_kernel, out_shape=[jax.ShapeDtypeStruct((OWN,) + s...  126 us
    unnamed x3, local copies, waits for them, and re-layouts  4.81 us

profile of v3, /device:TPU:1, one launch (start us, length us, event | category | flops | bytes accessed | tf_op | source)
XLA Modules:
  0.0 131.8 jit_solution(13006245534238812763)
XLA Ops:
  1.3 125.7 %node_basis.1 = (f32[8,128,128]{2,1,0:T(8,128)}, f32[128,128]{1,0:T(8,128)}, f32[128,128]{1,0:T(8,128)}) custom-call(s32[1,1]{1,0:T(1,128)S(6)} %copy.11.count, s32[1,320]{1,0:T(1,128)} %bitcast.8, s32[1,320]{1,0:T(1,128)} %bitcast.9, f32[320,128,128]{2,1,0:T(8,128)} %bitcast.5, f32[8,128,128]{2,1,0:T(8,128)} %bitcast.6), custom_call_target="tpu_custom_call" | custom-call | tf_op jit(solution)/shard_map/node_basis/pallas_call | solution.py:435
  127.0 1.9 %copy.12 = f32[1024,128]{1,0:T(8,128)} copy(f32[1024,128]{1,0:T(8,128)} %bitcast.7) | data formatting | bytes 1048576
  128.9 1.5 %copy.13 = f32[128,128]{1,0:T(8,128)} copy(f32[128,128]{1,0:T(8,128)} %get-tuple-element.13) | data formatting | bytes 131072
  130.4 1.5 %copy.14 = f32[128,128]{1,0:T(8,128)} copy(f32[128,128]{1,0:T(8,128)} %get-tuple-element.14) | data formatting | bytes 131072

commit v4 on v3

--- a/solution.py
+++ b/solution.py
@@ -18,6 +18,7 @@
 STAGE = 8
 STRIP = 16
 SLICE = TILE // N_COLS
+SPREAD = 1.5
 NODES = OWN * TILE * N_ROWS * N_COLS
 SLOTS = 8
 MESH = pl.DeviceIdType.MESH
@@ -123,7 +124,7 @@
 
 
 def product_kernel(
-    count, rows_idx, cols_idx, tiles, probes, basis, factor, first_factor,
+    count, rows_idx, cols_idx, tiles, probes, plain, scaled, upper, inverse, health,
     own, gx, pairs, stage, xpair, sums, panel, near, mid, far,
     plan, table, mats, share, slices, grams, got_cols, got_rows, work, uppers, lowers,
     stage_sem, sa, ra, sb, rb, sc, rc, sd, rd, se, re, sf, rf, sg, rg,
@@ -169,6 +170,7 @@
 
     def turned(b, carry):
         block = jnp.transpose(probes[b])
+        mats[0, b] = block
         for j in range(PARTS):
             own[j, b] = block[j * WIDTH:(j + 1) * WIDTH]
             gx[j, y, z, b] = block[j * WIDTH:(j + 1) * WIDTH]
@@ -184,50 +186,62 @@
     def step_of(s):
         return 1 if s == 0 else -1
 
-    def copy_a(j, h, s):
-        return remote(own.at[j, pl.ds(4 * h, 4)], gx.at[j, y, z, pl.ds(4 * h, 4)],
-                      sa.at[j, h, s], ra.at[j, h, s], row_peer(1 - h, step_of(s)))
+    def half(h, s, f):
+        return pl.ds(4 * h + 2 * (s if f == 0 else 1 - s), 2)
+
+    def copy_a(j, h, s, f):
+        cut = half(h, s, f)
+        return remote(own.at[j, cut], gx.at[j, y, z, cut],
+                      sa.at[j, h, s, f], ra.at[j, h, s, f], row_peer(1 - h, step_of(s)))
 
     def copy_b(j, h, s):
         yy, zz = yz(1 - h, -step_of(s))
-        ref = gx.at[j, yy, zz, pl.ds(4 * h + 2 * s, 2)]
+        ref = gx.at[j, yy, zz, half(h, s, 0)]
         return remote(ref, ref, sb.at[j, h, s], rb.at[j, h, s], row_peer(1 - h, step_of(s)))
 
-    def copy_c(j, h, s):
-        ref = gx.at[j, y, :, pl.ds(4 * h, 4)] if h == 0 else gx.at[j, :, z, pl.ds(4 * h, 4)]
-        return remote(ref, ref, sc.at[j, h, s], rc.at[j, h, s], row_peer(h, step_of(s)))
+    def copy_c(j, h, s, f):
+        cut = half(h, s, f)
+        ref = gx.at[j, y, :, cut] if h == 0 else gx.at[j, :, z, cut]
+        return remote(ref, ref, sc.at[j, h, s, f], rc.at[j, h, s, f], row_peer(h, step_of(s)))
 
     def copy_d(j, h, s):
         yy, zz = yz(h, -step_of(s))
-        cut = pl.ds(4 * h + 2 * s, 2)
+        cut = half(h, s, 0)
         ref = gx.at[j, yy, :, cut] if h == 0 else gx.at[j, :, zz, cut]
         return remote(ref, ref, sd.at[j, h, s], rd.at[j, h, s], row_peer(h, step_of(s)))
 
     ways = [(h, s) for h in (0, 1) for s in (0, 1)]
 
     def do_a(j):
-        for h, s in ways:
-            copy_a(j, h, s).start()
+        for f in (0, 1):
+            for h, s in ways:
+                copy_a(j, h, s, f).start()
 
     def do_b(j):
         for h, s in ways:
-            copy_a(j, h, s).wait_recv()
+            copy_a(j, h, s, 0).wait_recv()
             copy_b(j, h, s).start()
 
     def do_c(j):
-        for h in (0, 1):
-            copy_b(j, h, 0).wait_recv()
-            copy_b(j, h, 1).wait_recv()
-            copy_c(j, h, 0).start()
-            copy_c(j, h, 1).start()
+        for h, s in ways:
+            copy_a(j, h, s, 1).wait_recv()
+        for h, s in ways:
+            copy_b(j, h, s).wait_recv()
+        for h, s in ways:
+            copy_c(j, h, s, 0).start()
+
+    def do_cc(j):
+        for h, s in ways:
+            copy_c(j, h, s, 1).start()
 
     def do_d(j):
         for h, s in ways:
-            copy_c(j, h, s).wait_recv()
+            copy_c(j, h, s, 0).wait_recv()
             copy_d(j, h, s).start()
 
     def do_e(j):
         for h, s in ways:
+            copy_c(j, h, s, 1).wait_recv()
             copy_d(j, h, s).wait_recv()
 
     def split(i, carry):
@@ -275,29 +289,37 @@
 
         lax.fori_loop(0, PANEL, one, 0, unroll=8)
 
-    def swap(j):
-        return remote(panel.at[j, :, 1 - q], near.at[j], se.at[j], re.at[j], partner)
+    def swap(j, off):
+        at = turn(x, off)
+        i = off % SIDE
+        return remote(panel.at[j, at, 1 - q], near.at[j, at], se.at[j, i], re.at[j, i], partner)
 
     def copy_f(j, s):
         return remote(panel.at[j, turn(x, 2), q, pl.ds(4 * s, 4)], mid.at[j, s],
                       sf.at[j, s], rf.at[j, s], x_peer(step_of(s)))
 
-    def copy_g(j, s):
-        return remote(panel.at[j, turn(x, step_of(s)), q], far.at[j, s],
-                      sg.at[j, s], rg.at[j, s], x_peer(step_of(s)))
+    def copy_g(j, s, f):
+        cut = pl.ds(4 * (1 - s if f == 0 else s), 4)
+        return remote(panel.at[j, turn(x, step_of(s)), q, cut], far.at[j, s, cut],
+                      sg.at[j, s, f], rg.at[j, s, f], x_peer(step_of(s)))
+
+    offs = (2, 1, -1, 0)
 
     def do_p(j):
         collect(j)
-        swap(j).start()
+        for off in offs:
+            swap(j, off).start()
 
     def do_q(j):
-        swap(j).wait_recv()
-        for off in (2, 1, -1, 0):
+        for off in offs:
+            swap(j, off).wait_recv()
             at = turn(x, off)
             panel[j, at, q] = panel[j, at, q] + near[j, at]
             if off == 2:
                 copy_f(j, 0).start()
                 copy_f(j, 1).start()
+            elif off != 0:
+                copy_g(j, 0 if off == 1 else 1, 0).start()
 
     def do_r(j):
         for s in (0, 1):
@@ -305,62 +327,13 @@
             at = turn(x, step_of(s))
             cut = pl.ds(4 * s, 4)
             panel[j, at, q, cut] = panel[j, at, q, cut] + mid[j, s]
-            copy_g(j, s).start()
+            copy_g(j, s, 1).start()
 
     def do_s(j):
-        copy_g(j, 0).wait_recv()
-        copy_g(j, 1).wait_recv()
-        mats[0, :, j * WIDTH:(j + 1) * WIDTH, :] = panel[j, x, q] + (far[j, 0] + far[j, 1])
-
-    steps = CAP // STAGE
-
-    def some(lo, hi):
-        lax.fori_loop(lo, hi, split, 0)
-
-    for j in range(PARTS):
-        do_a(j)
-    sort_slots(count[0, 0], rows_idx, cols_idx, plan)
-    to_scalars = pltpu.make_async_copy(plan, table, table_sem)
-    to_scalars.start()
-    some(0, 3)
-    do_b(0)
-    some(3, 6)
-    do_b(1)
-    some(6, 9)
-    do_b(2)
-    do_c(0)
-    some(9, 14)
-    do_b(3)
-    do_c(1)
-    some(14, 26)
-    do_d(0)
-    do_c(2)
-    some(26, steps)
-    to_scalars.wait()
-    do_e(0)
-
-    zero = jnp.zeros((WIDTH, TILE), jnp.float32)
-    cuts = (0, 64, 160, 224, 320)
-
-    def part(j, between):
-        spread(j)
-        run = zero
-        for k in range(4):
-            run = multiply(cuts[k], cuts[k + 1] - cuts[k], run)
-            for act, i in between[k]:
-                act(i)
-
-    part(0, [[(do_d, 1), (do_c, 3)], [], [], [(do_p, 0)]])
-    do_e(1)
-    part(1, [[(do_q, 0)], [(do_d, 2)], [], [(do_r, 0), (do_p, 1)]])
-    do_e(2)
-    part(2, [[(do_d, 3)], [(do_q, 1), (do_s, 0)], [], [(do_r, 1), (do_p, 2)]])
-    do_e(3)
-    part(3, [[], [(do_q, 2), (do_s, 1)], [], [(do_r, 2), (do_p, 3)]])
-    do_q(3)
-    do_s(2)
-    do_r(3)
-    do_s(3)
+        for s in (0, 1):
+            for f in (0, 1):
+                copy_g(j, s, f).wait_recv()
+        mats[1, :, j * WIDTH:(j + 1) * WIDTH, :] = panel[j, x, q] + (far[j, 0] + far[j, 1])
 
     def copy_h(p, d):
         to = lax.rem(c + d, N_COLS)
@@ -372,14 +345,16 @@
     def copy_j(p, d):
         return remote(grams.at[p, c], grams.at[p, c], sj.at[p, d], rj.at[p, d], col_mate(d))
 
-    def orthogonal(p, carry):
+    def sum_start(p, at):
         total = jnp.zeros((TILE, TILE), jnp.float32)
         for b in range(OWN):
-            block = mats[p, b]
+            block = mats[at, b]
             total = total + exact(block, block, 1, 1)
         share[p] = total.reshape(N_COLS, SLICE, TILE)
         for d in range(1, N_COLS):
             copy_h(p, d).start()
+
+    def sum_rows(p):
         for d in range(1, N_COLS):
             copy_h(p, d).wait_recv()
         part = share[p, c]
@@ -389,6 +364,8 @@
         got_rows[p, r] = part
         for d in range(1, N_ROWS):
             copy_i(p, d).start()
+
+    def sum_cols(p):
         for d in range(1, N_ROWS):
             copy_i(p, d).wait_recv()
         part = got_rows[p, 0]
@@ -397,32 +374,110 @@
         grams[p, c] = part
         for d in range(1, N_COLS):
             copy_j(p, d).start()
+
+    def sum_end(p):
         for d in range(1, N_COLS):
             copy_j(p, d).wait_recv()
         triangles(grams[p].reshape(TILE, TILE) / NODES, uppers.at[p], lowers.at[p], work)
-        lower = lowers[p]
-        for b in range(OWN):
-            mats[p + 1, b] = exact(lower, mats[p, b], 1, 0)
+
+    steps = CAP // STAGE
+
+    def some(lo, hi):
+        lax.fori_loop(lo, hi, split, 0)
+
+    for j in range(PARTS):
+        do_a(j)
+    sum_start(0, 0)
+    sort_slots(count[0, 0], rows_idx, cols_idx, plan)
+    to_scalars = pltpu.make_async_copy(plan, table, table_sem)
+    to_scalars.start()
+    do_b(0)
+    do_b(1)
+    sum_rows(0)
+    some(0, 4)
+    do_b(2)
+    do_b(3)
+    do_c(0)
+    do_cc(0)
+    do_c(1)
+    some(4, 16)
+    sum_cols(0)
+    some(16, 26)
+    do_d(0)
+    do_cc(1)
+    do_c(2)
+    some(26, steps)
+    to_scalars.wait()
+    sum_end(0)
+    do_d(1)
+    do_cc(2)
+    do_c(3)
+    do_e(0)
+
+    zero = jnp.zeros((WIDTH, TILE), jnp.float32)
+    cuts = (0, 64, 160, 224, 320)
+
+    def part(j, between):
+        spread(j)
+        run = zero
+        for k in range(4):
+            run = multiply(cuts[k], cuts[k + 1] - cuts[k], run)
+            for act, i in between[k]:
+                act(i)
+
+    part(0, [[], [], [], [(do_p, 0), (do_d, 2), (do_cc, 3)]])
+    do_e(1)
+    part(1, [[], [(do_q, 0)], [], [(do_r, 0), (do_d, 3), (do_p, 1)]])
+    do_e(2)
+    part(2, [[], [(do_q, 1), (do_s, 0)], [], [(do_r, 1), (do_p, 2)]])
+    do_e(3)
+    part(3, [[], [(do_q, 2), (do_s, 1)], [], [(do_r, 2), (do_p, 3)]])
+    do_q(3)
+    do_s(2)
+    do_r(3)
+    do_s(3)
+
+    lower = lowers[0]
+    for b in range(OWN):
+        mats[2, b] = exact(lower, mats[1, b], 1, 0)
+    sum_start(1, 2)
+    sum_rows(1)
+    sum_cols(1)
+    sum_end(1)
+    plain[...] = mats[1]
+    scaled[...] = mats[2]
+    upper[...] = uppers[...]
+    inverse[...] = lowers[1]
+    spread_of = jnp.sum(jnp.square(uppers[1]), keepdims=True) * jnp.sum(jnp.square(lowers[1]), keepdims=True)
+    health[...] = jnp.broadcast_to(spread_of / (TILE * TILE), (8, TILE))
+
+    for j in range(PARTS):
+        for h, s in ways:
+            for f in (0, 1):
+                copy_a(j, h, s, f).wait_send()
+                copy_c(j, h, s, f).wait_send()
+            copy_b(j, h, s).wait_send()
+            copy_d(j, h, s).wait_send()
+        for off in offs:
+            swap(j, off).wait_send()
+        for s in (0, 1):
+            copy_f(j, s).wait_send()
+            copy_g(j, s, 0).wait_send()
+            copy_g(j, s, 1).wait_send()
+    for p in (0, 1):
         for d in range(1, N_COLS):
             copy_h(p, d).wait_send()
             copy_j(p, d).wait_send()
         for d in range(1, N_ROWS):
             copy_i(p, d).wait_send()
-        return carry
-
-    lax.fori_loop(0, 2, orthogonal, 0)
+
+
+def finish_kernel(scaled, upper, inverse, basis, factor, first_factor):
     for b in range(OWN):
-        basis[b] = jnp.transpose(mats[2, b])
-    first_factor[...] = uppers[0]
-    factor[...] = exact(uppers[1], uppers[0], 1, 0)
-    for j in range(PARTS):
-        for h, s in ways:
-            for copy in (copy_a, copy_b, copy_c, copy_d):
-                copy(j, h, s).wait_send()
-        swap(j).wait_send()
-        for s in (0, 1):
-            copy_f(j, s).wait_send()
-            copy_g(j, s).wait_send()
+        basis[b] = jnp.transpose(exact(inverse[...], scaled[b], 1, 0))
+    whole = exact(upper[1], upper[0], 1, 0)
+    factor[...] = whole
+    first_factor[...] = whole
 
 
 def product(tiles, rows_idx, cols_idx, count, probes):
@@ -436,11 +491,13 @@
         product_kernel,
         out_shape=[
             jax.ShapeDtypeStruct((OWN,) + square, f32),
+            jax.ShapeDtypeStruct((OWN,) + square, f32),
+            jax.ShapeDtypeStruct((2,) + square, f32),
             jax.ShapeDtypeStruct(square, f32),
-            jax.ShapeDtypeStruct(square, f32),
+            jax.ShapeDtypeStruct((8, TILE), f32),
         ],
         in_specs=[scalar, vector, vector, pl.BlockSpec(memory_space=pl.ANY), vector],
-        out_specs=[vector] * 3,
+        out_specs=[vector] * 5,
         scratch_shapes=[
             pltpu.VMEM((PARTS,) + piece, f32),
             pltpu.VMEM((PARTS, SIDE, SIDE) + piece, f32),
@@ -465,9 +522,13 @@
             pltpu.VMEM((2,) + square, f32),
             DMA((SLOTS,)),
         ]
-        + [DMA((PARTS, 2, 2))] * 8
-        + [DMA((PARTS,))] * 2
-        + [DMA((PARTS, 2))] * 4
+        + [DMA((PARTS, 2, 2, 2))] * 2
+        + [DMA((PARTS, 2, 2))] * 2
+        + [DMA((PARTS, 2, 2, 2))] * 2
+        + [DMA((PARTS, 2, 2))] * 2
+        + [DMA((PARTS, SIDE))] * 2
+        + [DMA((PARTS, 2))] * 2
+        + [DMA((PARTS, 2, 2))] * 2
         + [DMA(())]
         + [DMA((2, N_COLS))] * 2
         + [DMA((2, N_ROWS))] * 2
@@ -478,10 +539,126 @@
     )(count, rows_idx, cols_idx, tiles, probes.reshape((OWN,) + square))
 
 
+def finish(scaled, upper, inverse):
+    vector = pl.BlockSpec(memory_space=pltpu.VMEM)
+    square = jax.ShapeDtypeStruct((TILE, TILE), jnp.float32)
+    return pl.pallas_call(
+        finish_kernel,
+        out_shape=[jax.ShapeDtypeStruct(scaled.shape, jnp.float32), square, square],
+        in_specs=[vector] * 3,
+        out_specs=[vector] * 3,
+        compiler_params=pltpu.CompilerParams(vmem_limit_bytes=16 * 2**20),
+        name="finish",
+    )(scaled, upper, inverse)
+
+
+def signal_all(sem, r, c):
+    def cols_peer(d, carry):
+        pl.semaphore_signal(sem, inc=1, device_id=(r, lax.rem(c + d, N_COLS)), device_id_type=MESH)
+        return carry
+
+    def rows_peer(d, carry):
+        pl.semaphore_signal(sem, inc=1, device_id=(lax.rem(r + d, N_ROWS), c), device_id_type=MESH)
+        return carry
+
+    lax.fori_loop(1, N_COLS, cols_peer, 0)
+    lax.fori_loop(1, N_ROWS, rows_peer, 0)
+
+
+def sum_kernel(g_ref, out_ref, part, got_a, got_b, send_a, recv_a, send_b, recv_b, send_c, recv_c):
+    r, c = lax.axis_index("rows"), lax.axis_index("cols")
+    barrier = pltpu.get_barrier_semaphore()
+    signal_all(barrier, r, c)
+    pl.semaphore_wait(barrier, N_COLS - 1 + N_ROWS - 1)
+
+    def copy_a(d):
+        to = lax.rem(c + d, N_COLS)
+        return pltpu.make_async_remote_copy(
+            src_ref=g_ref.at[to], dst_ref=got_a.at[d], send_sem=send_a.at[d], recv_sem=recv_a.at[d],
+            device_id=(r, to), device_id_type=MESH)
+
+    def copy_b(d):
+        return pltpu.make_async_remote_copy(
+            src_ref=part, dst_ref=got_b.at[r], send_sem=send_b.at[d], recv_sem=recv_b.at[d],
+            device_id=(lax.rem(r + d, N_ROWS), c), device_id_type=MESH)
+
+    def copy_c(d):
+        return pltpu.make_async_remote_copy(
+            src_ref=out_ref.at[c], dst_ref=out_ref.at[c], send_sem=send_c.at[d], recv_sem=recv_c.at[d],
+            device_id=(r, lax.rem(c + d, N_COLS)), device_id_type=MESH)
+
+    def each(copy, n, act):
+        def step(d, carry):
+            getattr(copy(d), act)()
+            return carry
+
+        lax.fori_loop(1, n, step, 0)
+
+    each(copy_a, N_COLS, "start")
+    each(copy_a, N_COLS, "wait_recv")
+    total = g_ref[c]
+    for d in range(1, N_COLS):
+        total = total + got_a[d]
+    part[...] = total
+    got_b[r] = total
+    each(copy_b, N_ROWS, "start")
+    each(copy_a, N_COLS, "wait_send")
+    each(copy_b, N_ROWS, "wait_recv")
+    total = got_b[0]
+    for d in range(1, N_ROWS):
+        total = total + got_b[d]
+    out_ref[c] = total
+    each(copy_c, N_COLS, "start")
+    each(copy_b, N_ROWS, "wait_send")
+    each(copy_c, N_COLS, "wait")
+
+
+def sum_everywhere(matrix, ident):
+    size = matrix.shape[0]
+    rows = size // N_COLS
+    piece = (rows, size)
+    out = pl.pallas_call(
+        sum_kernel,
+        out_shape=jax.ShapeDtypeStruct((N_COLS,) + piece, jnp.float32),
+        in_specs=[pl.BlockSpec(memory_space=pltpu.VMEM)],
+        out_specs=pl.BlockSpec(memory_space=pltpu.VMEM),
+        scratch_shapes=[
+            pltpu.VMEM(piece, jnp.float32),
+            pltpu.VMEM((N_COLS,) + piece, jnp.float32),
+            pltpu.VMEM((N_ROWS,) + piece, jnp.float32),
+            DMA((N_COLS,)), DMA((N_COLS,)), DMA((N_ROWS,)), DMA((N_ROWS,)), DMA((N_COLS,)), DMA((N_COLS,)),
+        ],
+        compiler_params=pltpu.CompilerParams(collective_id=ident, has_side_effects=True),
+        name="sum_everywhere",
+    )(matrix.reshape((N_COLS,) + piece))
+    return out.reshape(size, size)
+
+
+def two_passes(matrix):
+    def normal(value):
+        gram = jnp.einsum("rk,rl->kl", value, value, precision=lax.Precision.HIGHEST)
+        lower = jnp.linalg.cholesky(sum_everywhere(gram, 1) / NODES)
+        inverse = jax.scipy.linalg.solve_triangular(
+            lower, jnp.eye(TILE, dtype=jnp.float32), lower=True)
+        return jnp.dot(value, inverse.T, precision=lax.Precision.HIGHEST), lower
+
+    first, lower = normal(matrix)
+    basis, lower_next = normal(first)
+    return basis, jnp.dot(lower_next.T, lower.T, precision=lax.Precision.HIGHEST), lower.T
+
+
 def shards(tile_values, tile_rows, tile_cols, tile_count, probes):
-    basis, factor, first_factor = product(
+    plain, scaled, upper, inverse, health = product(
         tile_values[0, 0], tile_rows[0], tile_cols[0], tile_count, probes)
-    return basis.reshape(probes.shape), factor, first_factor
+
+    def well():
+        basis, factor, first_factor = finish(scaled, upper, inverse)
+        return basis.reshape(probes.shape), factor, first_factor
+
+    def ill():
+        return two_passes(jnp.swapaxes(plain, 1, 2).reshape(probes.shape))
+
+    return lax.cond(health[0, 0] < SPREAD, well, ill)
 
 
 def solution(mesh):

time: 132 us -> 106 us (0.80)
  Pallas kernels: 126 us -> 103 us
  local copies, waits for them, and re-layouts: 4.81 us -> 1.19 us
    pallas_call x1, Pallas kernels: 126 us -> 101 us  [product(): pl.pallas_call(product_kernel, out_shape=[jax.ShapeDtypeStruct((OWN,) + s...]
    unnamed x3 -> x0, local copies, waits for them, and re-layouts: 4.81 us -> none
    pallas_call x0 -> x1, Pallas kernels: none -> 1.53 us  [finish(): pl.pallas_call(finish_kernel, out_shape=[jax.ShapeDtypeStruct(scaled.shap...]
where the time goes in v4:
time: 106 us
  Pallas kernels  103 us (97%)
  between operations  1.94 us (2%)
  local copies, waits for them, and re-layouts  1.19 us (1%)
    pallas_call x1, Pallas kernels, product(): pl.pallas_call(product_kernel, out_shape=[jax.ShapeDtypeStruct((OWN,) + s...  101 us

profile of v4, /device:TPU:1, one launch (start us, length us, event | category | flops | bytes accessed | tf_op | source)
XLA Modules:
  0.0 106.2 jit_solution(5427624463814924057)
XLA Ops:
  1.3 101.2 %node_basis.1 = (f32[8,128,128]{2,1,0:T(8,128)S(1)}, f32[8,128,128]{2,1,0:T(8,128)S(1)}, f32[2,128,128]{2,1,0:T(8,128)S(1)}, f32[128,128]{1,0:T(8,128)S(1)}, f32[8,128]{1,0:T(8,128)}) custom-call(s32[1,1]{1,0:T(1,128)S(6)} %copy.35.count, s32[1,320]{1,0:T(1,128)} %bitcast.57, s32[1,320]{1,0:T(1,128)} %bitcast.58, f32[320,128,128]{2,1,0:T(8,128)} %bitcast.47, ...), custom_call_target="tpu_custom_call" | custom-call | tf_op jit(solution)/shard_map/node_basis/pallas_call | solution.py:490
  102.5 1.2 %slice.11 = f32[1,1]{1,0:T(1,128)} slice(f32[8,128]{1,0:T(8,128)} %get-tuple-element.23), slice={[0:1], [0:1]} | slice | bytes 8 | tf_op jit(solution)/shard_map/slice | solution.py:661
  104.4 1.8 %conditional.1 = (f32[1024,128]{1,0:T(8,128)}, f32[128,128]{1,0:T(8,128)}, f32[128,128]{1,0:T(8,128)}) conditional(s32[]{:T(128)} %bitcast.21, f32[8,128,128]{2,1,0:T(8,128)S(1)} %get-tuple-element.24, (f32[8,128,128]{2,1,0:T(8,128)S(1)}, f32[2,128,128]{2,1,0:T(8,128)S(1)}, f32[128,128]{1,0:T(8,128)S(1)}) %tuple.17), branch_computations={%region_0.5_spmd, %region_3.6_spmd} | conditional | flops 881295616 | bytes 7997470 | solution.py:661
  104.6 1.5 %finish.1 = (f32[8,128,128]{2,1,0:T(8,128)}, f32[128,128]{1,0:T(8,128)}, f32[128,128]{1,0:T(8,128)}) custom-call(f32[8,128,128]{2,1,0:T(8,128)S(1)} %get-tuple-element.6.scaled, f32[2,128,128]{2,1,0:T(8,128)S(1)} %get-tuple-element.10.upper, f32[128,128]{1,0:T(8,128)S(1)} %get-tuple-element.11.inverse), custom_call_target="tpu_custom_call" | custom-call | tf_op jit(solution)/shard_map/cond/branch_1_fun/finish/pallas_call | solution.py:545

commit v5 on v4

--- a/solution.py
+++ b/solution.py
@@ -14,7 +14,7 @@
 PANEL = OWN * N_COLS
 PARTS = 4
 WIDTH = TILE // PARTS
-GROUP = 32
+GROUP = 40
 STAGE = 8
 STRIP = 16
 SLICE = TILE // N_COLS
@@ -124,11 +124,11 @@
 
 
 def product_kernel(
-    count, rows_idx, cols_idx, tiles, probes, plain, scaled, upper, inverse, health,
-    own, gx, pairs, stage, xpair, sums, panel, near, mid, far,
+    count_in, rows_in, cols_in, tiles, probes_in, plain, scaled, upper, inverse, health,
+    count, rows_idx, cols_idx, probes, own, gx, pairs, stage, xpair, sums, panel, near, mid, far,
     plan, table, mats, share, slices, grams, got_cols, got_rows, work, uppers, lowers,
     stage_sem, sa, ra, sb, rb, sc, rc, sd, rd, se, re, sf, rf, sg, rg,
-    table_sem, sh, rh, si, ri, sj, rj,
+    table_sem, in_sem, out_sem, sh, rh, si, ri, sj, rj,
 ):
     r, c = lax.axis_index("rows"), lax.axis_index("cols")
     y, z = r // SIDE, lax.rem(r, SIDE)
@@ -152,8 +152,13 @@
     def load(i, slot):
         return pltpu.make_async_copy(tiles.at[pl.ds(i * STAGE, STAGE)], stage.at[slot], stage_sem.at[slot])
 
-    for i in range(SLOTS):
-        load(i, i).start()
+    fetch = [
+        pltpu.make_async_copy(src, dst, in_sem.at[i])
+        for i, (src, dst) in enumerate(
+            [(probes_in, probes), (rows_in, rows_idx), (cols_in, cols_idx), (count_in, count)])
+    ]
+    for copy in fetch:
+        copy.start()
 
     barrier = pltpu.get_barrier_semaphore()
 
@@ -167,6 +172,9 @@
         pl.semaphore_signal(barrier, inc=1, device_id=col_mate(d), device_id_type=MESH)
     for d in range(1, N_ROWS):
         pl.semaphore_signal(barrier, inc=1, device_id=row_mate(d), device_id_type=MESH)
+
+    for i in range(SLOTS):
+        load(i, i).start()
 
     def turned(b, carry):
         block = jnp.transpose(probes[b])
@@ -176,6 +184,7 @@
             gx[j, y, z, b] = block[j * WIDTH:(j + 1) * WIDTH]
         return carry
 
+    fetch[0].wait()
     lax.fori_loop(0, OWN, turned, 0)
     pl.semaphore_wait(barrier, N_COLS - 1 + N_ROWS - 1)
 
@@ -388,6 +397,8 @@
     for j in range(PARTS):
         do_a(j)
     sum_start(0, 0)
+    for copy in fetch[1:]:
+        copy.wait()
     sort_slots(count[0, 0], rows_idx, cols_idx, plan)
     to_scalars = pltpu.make_async_copy(plan, table, table_sem)
     to_scalars.start()
@@ -415,7 +426,7 @@
     do_e(0)
 
     zero = jnp.zeros((WIDTH, TILE), jnp.float32)
-    cuts = (0, 64, 160, 224, 320)
+    cuts = (0, 80, 160, 240, 320)
 
     def part(j, between):
         spread(j)
@@ -425,13 +436,18 @@
             for act, i in between[k]:
                 act(i)
 
-    part(0, [[], [], [], [(do_p, 0), (do_d, 2), (do_cc, 3)]])
+    part(0, [[], [], [], [(do_p, 0)]])
+    do_d(2)
+    do_cc(3)
     do_e(1)
-    part(1, [[], [(do_q, 0)], [], [(do_r, 0), (do_d, 3), (do_p, 1)]])
+    part(1, [[], [(do_q, 0)], [], [(do_p, 1)]])
+    do_d(3)
+    do_r(0)
     do_e(2)
-    part(2, [[], [(do_q, 1), (do_s, 0)], [], [(do_r, 1), (do_p, 2)]])
+    part(2, [[], [(do_q, 1)], [(do_s, 0)], [(do_p, 2)]])
+    do_r(1)
     do_e(3)
-    part(3, [[], [(do_q, 2), (do_s, 1)], [], [(do_r, 2), (do_p, 3)]])
+    part(3, [[], [(do_q, 2)], [(do_s, 1)], [(do_r, 2), (do_p, 3)]])
     do_q(3)
     do_s(2)
     do_r(3)
@@ -440,16 +456,22 @@
     lower = lowers[0]
     for b in range(OWN):
         mats[2, b] = exact(lower, mats[1, b], 1, 0)
+    store = [
+        pltpu.make_async_copy(mats.at[1], plain, out_sem.at[0]),
+        pltpu.make_async_copy(mats.at[2], scaled, out_sem.at[1]),
+    ]
+    for copy in store:
+        copy.start()
     sum_start(1, 2)
     sum_rows(1)
     sum_cols(1)
     sum_end(1)
-    plain[...] = mats[1]
-    scaled[...] = mats[2]
     upper[...] = uppers[...]
     inverse[...] = lowers[1]
     spread_of = jnp.sum(jnp.square(uppers[1]), keepdims=True) * jnp.sum(jnp.square(lowers[1]), keepdims=True)
-    health[...] = jnp.broadcast_to(spread_of / (TILE * TILE), (8, TILE))
+    health[0, 0] = jnp.where(spread_of[0, 0] < SPREAD * TILE * TILE, 1, 0)
+    for copy in store:
+        copy.wait()
 
     for j in range(PARTS):
         for h, s in ways:
@@ -483,6 +505,7 @@
 def product(tiles, rows_idx, cols_idx, count, probes):
     scalar = pl.BlockSpec(memory_space=pltpu.SMEM)
     vector = pl.BlockSpec(memory_space=pltpu.VMEM)
+    anywhere = pl.BlockSpec(memory_space=pl.ANY)
     f32, bf16 = jnp.float32, jnp.bfloat16
     piece = (OWN, WIDTH, TILE)
     square = (TILE, TILE)
@@ -494,11 +517,15 @@
             jax.ShapeDtypeStruct((OWN,) + square, f32),
             jax.ShapeDtypeStruct((2,) + square, f32),
             jax.ShapeDtypeStruct(square, f32),
-            jax.ShapeDtypeStruct((8, TILE), f32),
+            jax.ShapeDtypeStruct((1, 1), jnp.int32),
         ],
-        in_specs=[scalar, vector, vector, pl.BlockSpec(memory_space=pl.ANY), vector],
-        out_specs=[vector] * 5,
+        in_specs=[anywhere] * 5,
+        out_specs=[anywhere] * 2 + [vector] * 2 + [scalar],
         scratch_shapes=[
+            pltpu.SMEM((1, 1), jnp.int32),
+            pltpu.VMEM((1, CAP), jnp.int32),
+            pltpu.VMEM((1, CAP), jnp.int32),
+            pltpu.VMEM((OWN,) + square, f32),
             pltpu.VMEM((PARTS,) + piece, f32),
             pltpu.VMEM((PARTS, SIDE, SIDE) + piece, f32),
             pltpu.VMEM((CAP, 2 * TILE, TILE), bf16),
@@ -529,7 +556,7 @@
         + [DMA((PARTS, SIDE))] * 2
         + [DMA((PARTS, 2))] * 2
         + [DMA((PARTS, 2, 2))] * 2
-        + [DMA(())]
+        + [DMA(()), DMA((4,)), DMA((2,))]
         + [DMA((2, N_COLS))] * 2
         + [DMA((2, N_ROWS))] * 2
         + [DMA((2, N_COLS))] * 2,
@@ -658,7 +685,7 @@
     def ill():
         return two_passes(jnp.swapaxes(plain, 1, 2).reshape(probes.shape))
 
-    return lax.cond(health[0, 0] < SPREAD, well, ill)
+    return lax.cond(health[0, 0] != 0, well, ill)
 
 
 def solution(mesh):

time: 106 us -> 102 us (0.962)
  Pallas kernels: 103 us -> 100 us
  local copies, waits for them, and re-layouts: 1.19 us -> 0 us
    pallas_call x1, Pallas kernels: 101 us -> 98.4 us  [product(): pl.pallas_call(product_kernel, out_shape=[jax.ShapeDtypeStruct((OWN,) + s...]
    slice x1 -> x0, local copies, waits for them, and re-layouts: 1.19 us -> none  [shards(): return lax.cond(health[0, 0] < SPREAD, well, ill)]
where the time goes in v5:
time: 102 us
  Pallas kernels  100 us (98%)
  between operations  1.98 us (2%)
    pallas_call x1, Pallas kernels, product(): pl.pallas_call(product_kernel, out_shape=[jax.ShapeDtypeStruct((OWN,) + s...  98.4 us

profile of v5, /device:TPU:1, one launch (start us, length us, event | category | flops | bytes accessed | tf_op | source)
XLA Modules:
  0.0 102.2 jit_solution(5655764156789624090)
XLA Ops:
  1.3 98.4 %node_basis.1 = (f32[8,128,128]{2,1,0:T(8,128)S(1)}, f32[8,128,128]{2,1,0:T(8,128)S(1)}, f32[2,128,128]{2,1,0:T(8,128)S(1)}, f32[128,128]{1,0:T(8,128)S(1)}, s32[1,1]{1,0:T(1,128)}) custom-call(s32[1,1]{1,0:T(1,128)S(6)} %copy.35.count_in, s32[1,320]{1,0:T(1,128)} %bitcast.57, s32[1,320]{1,0:T(1,128)} %bitcast.58, f32[320,128,128]{2,1,0:T(8,128)} %bitcast.47, ...), custom_call_target="tpu_custom_call" | custom-call | tf_op jit(solution)/shard_map/node_basis/pallas_call | solution.py:513
  100.4 1.8 %conditional.1 = (f32[1024,128]{1,0:T(8,128)}, f32[128,128]{1,0:T(8,128)}, f32[128,128]{1,0:T(8,128)}) conditional(s32[]{:T(128)} %bitcast.21, f32[8,128,128]{2,1,0:T(8,128)S(1)} %get-tuple-element.24, (f32[8,128,128]{2,1,0:T(8,128)S(1)}, f32[2,128,128]{2,1,0:T(8,128)S(1)}, f32[128,128]{1,0:T(8,128)S(1)}) %tuple.17), branch_computations={%region_0.5_spmd, %region_3.6_spmd} | conditional | flops 881295616 | bytes 7997470 | solution.py:688
  100.7 1.5 %finish.1 = (f32[8,128,128]{2,1,0:T(8,128)}, f32[128,128]{1,0:T(8,128)}, f32[128,128]{1,0:T(8,128)}) custom-call(f32[8,128,128]{2,1,0:T(8,128)S(1)} %get-tuple-element.6.scaled, f32[2,128,128]{2,1,0:T(8,128)S(1)} %get-tuple-element.10.upper, f32[128,128]{1,0:T(8,128)S(1)} %get-tuple-element.11.inverse), custom_call_target="tpu_custom_call" | custom-call | tf_op jit(solution)/shard_map/cond/branch_1_fun/finish/pallas_call | solution.py:572

commit v6 on v5

--- a/solution.py
+++ b/solution.py
@@ -17,6 +17,7 @@
 GROUP = 40
 STAGE = 8
 STRIP = 16
+HEAD = TILE - WIDTH
 SLICE = TILE // N_COLS
 SPREAD = 1.5
 NODES = OWN * TILE * N_ROWS * N_COLS
@@ -37,14 +38,12 @@
         preferred_element_type=jnp.float32)
 
 
-def triangles(gram, upper, inverse, work):
+def triangles(work, upper, inverse, first, end):
     rows = lax.broadcasted_iota(jnp.int32, (TILE, TILE), 0)
     cols = lax.broadcasted_iota(jnp.int32, (TILE, TILE), 1)
-    work[:, 0:TILE] = gram
-    work[:, TILE:2 * TILE] = jnp.where(rows == cols, 1.0, 0.0)
     shape = (STRIP, TILE)
     place = lax.broadcasted_iota(jnp.int32, shape, 0)
-    for lo in range(0, TILE, STRIP):
+    for lo in range(first, end, STRIP):
         hi = lo + STRIP
         strip = work[lo:hi, 0:TILE]
         turned = work[lo:hi, TILE:2 * TILE]
@@ -65,6 +64,25 @@
         if hi < TILE:
             change = exact(strip, jnp.concatenate([strip, turned], axis=1), 0, 0)
             work[hi:, :] = work[hi:, :] - change[hi:, :]
+
+
+def with_identity(work, gram):
+    rows = lax.broadcasted_iota(jnp.int32, (TILE, TILE), 0)
+    cols = lax.broadcasted_iota(jnp.int32, (TILE, TILE), 1)
+    work[:, 0:TILE] = gram
+    work[:, TILE:2 * TILE] = jnp.where(rows == cols, 1.0, 0.0)
+
+
+def last_columns(work, upper, inverse, gram):
+    cols = lax.broadcasted_iota(jnp.int32, (HEAD, TILE), 1)
+    turned = inverse[0:HEAD, :]
+    side = jnp.where(cols >= HEAD, exact(turned, gram, 1, 0), 0.0)
+    upper[0:HEAD, :] = upper[0:HEAD, :] + side
+    change = exact(side, jnp.concatenate([side, turned], axis=1), 0, 0)
+    rows = lax.broadcasted_iota(jnp.int32, (TILE - HEAD, TILE), 0) + HEAD
+    below = lax.broadcasted_iota(jnp.int32, (TILE - HEAD, TILE), 1)
+    work[HEAD:, 0:TILE] = gram[HEAD:, :] - change[HEAD:, 0:TILE]
+    work[HEAD:, TILE:2 * TILE] = jnp.where(rows == below, 1.0, 0.0) - change[HEAD:, TILE:2 * TILE]
 
 
 def sort_slots(count, rows_idx, cols_idx, plan):
@@ -354,14 +372,21 @@
     def copy_j(p, d):
         return remote(grams.at[p, c], grams.at[p, c], sj.at[p, d], rj.at[p, d], col_mate(d))
 
-    def sum_start(p, at):
-        total = jnp.zeros((TILE, TILE), jnp.float32)
-        for b in range(OWN):
-            block = mats[at, b]
-            total = total + exact(block, block, 1, 1)
+    def sum_start(p, total):
         share[p] = total.reshape(N_COLS, SLICE, TILE)
         for d in range(1, N_COLS):
             copy_h(p, d).start()
+
+    def own_gram(at, first, end):
+        total = jnp.zeros((end - first, TILE), jnp.float32)
+        for b in range(OWN):
+            total = total + exact(mats[at, b, first:end, :], mats[at, b], 1, 1)
+        return total
+
+    def scale_rows(first, end):
+        lower = lowers[0, first:end, :]
+        for b in range(OWN):
+            mats[2, b, first:end, :] = exact(lower, mats[1, b], 1, 0)
 
     def sum_rows(p):
         for d in range(1, N_COLS):
@@ -387,7 +412,7 @@
     def sum_end(p):
         for d in range(1, N_COLS):
             copy_j(p, d).wait_recv()
-        triangles(grams[p].reshape(TILE, TILE) / NODES, uppers.at[p], lowers.at[p], work)
+        return grams[p].reshape(TILE, TILE) / NODES
 
     steps = CAP // STAGE
 
@@ -396,7 +421,9 @@
 
     for j in range(PARTS):
         do_a(j)
-    sum_start(0, 0)
+    sum_start(0, own_gram(0, 0, TILE))
+    mats[1, :, HEAD:, :] = jnp.zeros((OWN, WIDTH, TILE), jnp.float32)
+    mats[2, :, HEAD:, :] = jnp.zeros((OWN, WIDTH, TILE), jnp.float32)
     for copy in fetch[1:]:
         copy.wait()
     sort_slots(count[0, 0], rows_idx, cols_idx, plan)
@@ -419,7 +446,8 @@
     do_c(2)
     some(26, steps)
     to_scalars.wait()
-    sum_end(0)
+    with_identity(work, sum_end(0))
+    triangles(work, uppers.at[0], lowers.at[0], 0, TILE)
     do_d(1)
     do_cc(2)
     do_c(3)
@@ -450,22 +478,32 @@
     part(3, [[], [(do_q, 2)], [(do_s, 1)], [(do_r, 2), (do_p, 3)]])
     do_q(3)
     do_s(2)
+    scale_rows(0, HEAD)
+    blank = jnp.zeros((WIDTH, TILE), jnp.float32)
+    sum_start(1, jnp.concatenate([own_gram(2, 0, HEAD), blank], axis=0))
     do_r(3)
+    sum_rows(1)
     do_s(3)
-
-    lower = lowers[0]
-    for b in range(OWN):
-        mats[2, b] = exact(lower, mats[1, b], 1, 0)
+    scale_rows(HEAD, TILE)
+    low = own_gram(2, HEAD, TILE)
+    head = jnp.zeros((HEAD, TILE), jnp.float32)
+    low = jnp.concatenate([head, low], axis=0)
+    rows = lax.broadcasted_iota(jnp.int32, (TILE, TILE), 0)
+    sum_start(2, jnp.where(rows < HEAD, jnp.transpose(low), low))
     store = [
         pltpu.make_async_copy(mats.at[1], plain, out_sem.at[0]),
         pltpu.make_async_copy(mats.at[2], scaled, out_sem.at[1]),
     ]
     for copy in store:
         copy.start()
-    sum_start(1, 2)
-    sum_rows(1)
     sum_cols(1)
-    sum_end(1)
+    sum_rows(2)
+    with_identity(work, sum_end(1))
+    triangles(work, uppers.at[1], lowers.at[1], 0, HEAD // 2)
+    sum_cols(2)
+    triangles(work, uppers.at[1], lowers.at[1], HEAD // 2, HEAD)
+    last_columns(work, uppers.at[1], lowers.at[1], sum_end(2))
+    triangles(work, uppers.at[1], lowers.at[1], HEAD, TILE)
     upper[...] = uppers[...]
     inverse[...] = lowers[1]
     spread_of = jnp.sum(jnp.square(uppers[1]), keepdims=True) * jnp.sum(jnp.square(lowers[1]), keepdims=True)
@@ -486,7 +524,7 @@
             copy_f(j, s).wait_send()
             copy_g(j, s, 0).wait_send()
             copy_g(j, s, 1).wait_send()
-    for p in (0, 1):
+    for p in (0, 1, 2):
         for d in range(1, N_COLS):
             copy_h(p, d).wait_send()
             copy_j(p, d).wait_send()
@@ -539,11 +577,11 @@
             pltpu.VMEM((8, 3 * TILE), jnp.int32),
             pltpu.SMEM((8, 3 * TILE), jnp.int32),
             pltpu.VMEM((3, OWN) + square, f32),
-            pltpu.VMEM((2, N_COLS) + slab, f32),
-            pltpu.VMEM((2,) + slab, f32),
-            pltpu.VMEM((2, N_COLS) + slab, f32),
-            pltpu.VMEM((2, N_COLS) + slab, f32),
-            pltpu.VMEM((2, N_ROWS) + slab, f32),
+            pltpu.VMEM((3, N_COLS) + slab, f32),
+            pltpu.VMEM((3,) + slab, f32),
+            pltpu.VMEM((3, N_COLS) + slab, f32),
+            pltpu.VMEM((3, N_COLS) + slab, f32),
+            pltpu.VMEM((3, N_ROWS) + slab, f32),
             pltpu.VMEM((TILE, 2 * TILE), f32),
             pltpu.VMEM((2,) + square, f32),
             pltpu.VMEM((2,) + square, f32),
@@ -557,9 +595,9 @@
         + [DMA((PARTS, 2))] * 2
         + [DMA((PARTS, 2, 2))] * 2
         + [DMA(()), DMA((4,)), DMA((2,))]
-        + [DMA((2, N_COLS))] * 2
-        + [DMA((2, N_ROWS))] * 2
-        + [DMA((2, N_COLS))] * 2,
+        + [DMA((3, N_COLS))] * 2
+        + [DMA((3, N_ROWS))] * 2
+        + [DMA((3, N_COLS))] * 2,
         compiler_params=pltpu.CompilerParams(
             collective_id=2, has_side_effects=True, vmem_limit_bytes=60 * 2**20),
         name="node_basis",

time: 102 us -> 101 us (level)
  no operation moved by 1% of the time
where the time goes in v6:
time: 101 us
  Pallas kernels  99.1 us (98%)
  between operations  1.98 us (2%)
    pallas_call x1, Pallas kernels, product(): pl.pallas_call(product_kernel, out_shape=[jax.ShapeDtypeStruct((OWN,) + s...  97.5 us

profile of v6, /device:TPU:1, one launch (start us, length us, event | category | flops | bytes accessed | tf_op | source)
XLA Modules:
  0.0 101.3 jit_solution(13573257565283044101)
XLA Ops:
  1.3 97.5 %node_basis.1 = (f32[8,128,128]{2,1,0:T(8,128)S(1)}, f32[8,128,128]{2,1,0:T(8,128)S(1)}, f32[2,128,128]{2,1,0:T(8,128)S(1)}, f32[128,128]{1,0:T(8,128)S(1)}, s32[1,1]{1,0:T(1,128)}) custom-call(s32[1,1]{1,0:T(1,128)S(6)} %copy.35.count_in, s32[1,320]{1,0:T(1,128)} %bitcast.57, s32[1,320]{1,0:T(1,128)} %bitcast.58, f32[320,128,128]{2,1,0:T(8,128)} %bitcast.47, ...), custom_call_target="tpu_custom_call" | custom-call | tf_op jit(solution)/shard_map/node_basis/pallas_call | solution.py:551
  99.5 1.8 %conditional.1 = (f32[1024,128]{1,0:T(8,128)}, f32[128,128]{1,0:T(8,128)}, f32[128,128]{1,0:T(8,128)}) conditional(s32[]{:T(128)} %bitcast.21, f32[8,128,128]{2,1,0:T(8,128)S(1)} %get-tuple-element.24, (f32[8,128,128]{2,1,0:T(8,128)S(1)}, f32[2,128,128]{2,1,0:T(8,128)S(1)}, f32[128,128]{1,0:T(8,128)S(1)}) %tuple.17), branch_computations={%region_0.5_spmd, %region_3.6_spmd} | conditional | flops 881295616 | bytes 7997470 | solution.py:726
  99.8 1.5 %finish.1 = (f32[8,128,128]{2,1,0:T(8,128)}, f32[128,128]{1,0:T(8,128)}, f32[128,128]{1,0:T(8,128)}) custom-call(f32[8,128,128]{2,1,0:T(8,128)S(1)} %get-tuple-element.6.scaled, f32[2,128,128]{2,1,0:T(8,128)S(1)} %get-tuple-element.10.upper, f32[128,128]{1,0:T(8,128)S(1)} %get-tuple-element.11.inverse), custom_call_target="tpu_custom_call" | custom-call | tf_op jit(solution)/shard_map/cond/branch_1_fun/finish/pallas_call | solution.py:610
